TPU v7x, 128 devices: a whole 4x4x4 slice. The times are simulated.
128 devices in a mesh: grp: 4 (over z), blk: 32 (over y, x, core).
Axes of the slice: x: 4, y: 4, z: 4, core: 2. Of those that a mesh axis runs over, the one named last changes fastest.
Arguments:
- embeddings: bfloat16 [32768, 768], P(('grp', 'blk')), may hold values from -6 to 6
- target: int32 [32768, 1], P(('grp', 'blk')), may hold values from 0 to 127; in each aligned block of 256 rows (0 to 255, 256 to 511, ...) at most 4 rows name the same one
- cluster: int32 [32768], P(('grp', 'blk')), may hold values from 0 to 15
Outputs:
- nearest: float32 [32768], P(('grp', 'blk'))
Inputs may be any that keep to these rules, and one draw needn't show every extreme that they name: The rows of one device send at most 4 rows to any one target.
All inputs are finite; a program needn't handle non-finite values.
Results may differ from a plain program's by a relative error of at most 0.0014.
Values may be sent and summed in bfloat16 or wider, within the bound.
A program may use at most 64 MiB of HBM per device.

v0:
```python
import jax
import jax.numpy as jnp
from jax import lax
from jax.sharding import PartitionSpec as P


def normalize(embeddings):
    widened = embeddings.astype(jnp.float32)
    scale_inv = lax.rsqrt(jnp.sum(widened * widened, axis=1, keepdims=True) + 1e-06)
    return (widened * scale_inv).astype(jnp.bfloat16)


def compare(row_emb, row_ids, col_emb, col_ids, distinct):
    scores = lax.dot_general(
        row_emb, col_emb, (((1,), (1,)), ((), ())), preferred_element_type=jnp.float32
    )
    allowed = (row_ids[:, None] == col_ids[None, :]) & (row_ids[:, None] >= 0) & distinct
    masked = jnp.where(allowed, scores, -1.0)
    return (jnp.max(masked, axis=1), jnp.max(masked, axis=0))


def body(embeddings, target, cluster):
    devices_all = lax.axis_size(("grp", "blk"))
    rows_here = embeddings.shape[0]
    per_peer = max(2, 2 * rows_here // devices_all)
    slot_count = devices_all * per_peer
    target_dev = target[:, 0]
    order_ids = jnp.arange(rows_here)
    same_target = (target_dev[:, None] == target_dev[None, :]) & (
        order_ids[:, None] > order_ids[None, :]
    )
    slot_rank = jnp.sum(same_target.astype(jnp.int32), axis=1)
    slot_where = target_dev * per_peer + slot_rank
    normed = normalize(embeddings)
    width = normed.shape[1]
    send_rows = jnp.zeros((slot_count, width), jnp.bfloat16).at[slot_where].set(normed)
    send_ids = jnp.full((slot_count,), -1, jnp.int32).at[slot_where].set(cluster)
    own_rows, own_ids = (
        lax.all_to_all(send_rows, ("grp", "blk"), split_axis=0, concat_axis=0, tiled=True),
        lax.all_to_all(send_ids, ("grp", "blk"), split_axis=0, concat_axis=0, tiled=True),
    )
    own_pos = lax.axis_index("blk") * slot_count + jnp.arange(slot_count)
    piece_rows = lax.all_gather(own_rows, "blk", axis=0, tiled=True)
    piece_ids = lax.all_gather(own_ids, "blk", axis=0, tiled=True)
    length = piece_rows.shape[0]
    stacked_rows = piece_rows.reshape(length // slot_count, slot_count, width)
    stacked_ids = piece_ids.reshape(length // slot_count, slot_count)
    starts = slot_count * jnp.arange(length // slot_count)

    def one_block(acc, inputs):
        block_rows, block_ids, block_start = inputs
        col_pos = block_start + jnp.arange(slot_count)
        row_best, _ = compare(
            own_rows, own_ids, block_rows, block_ids, own_pos[:, None] != col_pos[None, :]
        )
        return (jnp.maximum(acc, row_best), None)

    best_next, _ = lax.scan(
        one_block, jnp.full((slot_count,), -1.0, jnp.float32), (stacked_rows, stacked_ids, starts)
    )
    back = lax.all_to_all(best_next, ("grp", "blk"), split_axis=0, concat_axis=0, tiled=True)
    return back[slot_where]


def solution(mesh):
    return jax.shard_map(
        body,
        mesh=mesh,
        in_specs=(P(("grp", "blk"), None), P(("grp", "blk"), None), P(("grp", "blk"))),
        out_specs=P(("grp", "blk")),
        check_vma=False,
    )
```

profile of v0, /device:TPU:1, one launch (start us, length us, event | category | flops | bytes accessed | tf_op | source)
XLA Modules:
  0.0 267.4 jit_solution(4432242986315225127)
XLA Ops:
  9.3 2.4 scatter_custom_fusion.1
  11.9 27.8 %all_to_all.36 = bf16[128,4,768]{2,1,0:T(4,128)(2,1)S(1)} all-to-all(bf16[128,4,768]{2,1,0:T(4,128)(2,1)S(1)} %all_to_all.27), channel_id=1, replica_groups=mesh['grp'=4,'blk'=32] {'grp','blk'}, dimensions={0} | all-to-all | bytes 1572864 | tf_op jit(solution)/shard_map/all_to_all | solution.py:39
  43.2 4.4 %all-to-all-start = ((s32[128,4,1]{1,2,0:T(1,128)}), s32[128,4,1]{1,2,0:T(1,128)S(1)}, u32[]{:S(2)}, u32[]{:S(2)}) async-start(s32[128,4,1]{1,2,0:T(1,128)} %bitcast.3), calls=%async_computation | async-start | bytes 131072 | tf_op jit(solution)/shard_map/all_to_all | solution.py:40
  47.7 9.6 %all-to-all-done = s32[128,4,1]{1,2,0:T(1,128)S(1)} async-done(((s32[128,4,1]{1,2,0:T(1,128)}), s32[128,4,1]{1,2,0:T(1,128)S(1)}, u32[]{:S(2)}, u32[]{:S(2)}) %all-to-all-start) | async-done | bytes 2080 | tf_op jit(solution)/shard_map/all_to_all | solution.py:40
  58.8 23.0 %all-gather = s32[32,1,512]{2,1,0:T(1,128)S(1)} all-gather(s32[1,1,512]{2,1,0:T(1,128)S(1)} %reshape.56), channel_id=1, replica_groups=mesh['grp'=4,'blk'=32] {'blk'}, dimensions={0}, use_global_device_ids=true | all-gather | bytes 67584 | tf_op jit(solution)/shard_map/all_gather | solution.py:44
  81.9 48.0 %all-gather.3.cloned.1.call-done = bf16[16384,768]{1,0:T(8,128)(2,1)} async-done(((bf16[512,768]{1,0:T(8,128)(2,1)}), bf16[16384,768]{1,0:T(8,128)(2,1)}) %all-gather.3.cloned.1.call-update) | async-done | bytes 25165840 | tf_op jit(solution)/shard_map/all_gather | solution.py:43
  129.8 109.1 %while.11 = (s32[]{:T(128)}, f32[512]{0:T(512)S(1)}, s32[512]{0:T(512)S(1)}, s32[32,512]{1,0:T(8,128)S(1)}, s32[32]{0:T(128)S(1)}, /*index=5*/bf16[32,512,768]{2...) while((s32[]{:T(128)}, f32[512]{0:T(512)S(1)}, s32[512]{0:T(512)S(1)}, ...), condition=%wide.region_6.7_spmd.clone, body=%wide.region_4.6_spmd.clone.sunk | while | flops 404228096 | bytes 1600659 | solution.py:58
  131.1 2.1 fusion.22
  134.5 2.1 fusion.22
  137.9 2.1 fusion.22
  141.3 2.1 fusion.22
  144.7 2.1 fusion.22
  148.2 2.1 fusion.22
  151.6 2.1 fusion.22
  155.0 2.1 fusion.22
  158.4 2.1 fusion.22
  161.8 2.1 fusion.22
  165.2 2.1 fusion.22
  168.6 2.1 fusion.22
  178.9 2.1 fusion.22
  182.3 2.1 fusion.22
  239.7 7.3 %all-to-all-start.2 = ((f32[128,4,1]{1,2,0:T(1,128)}), f32[128,4,1]{1,2,0:T(1,128)S(1)}, u32[]{:S(2)}, u32[]{:S(2)}) async-start(f32[128,4,1]{1,2,0:T(1,128)} %bitcast.5), calls=%async_computation.2 | async-start | bytes 131072 | tf_op jit(solution)/shard_map/all_to_all | solution.py:61
  247.0 9.6 %all-to-all-done.2 = f32[128,4,1]{1,2,0:T(1,128)S(1)} async-done(((f32[128,4,1]{1,2,0:T(1,128)}), f32[128,4,1]{1,2,0:T(1,128)S(1)}, u32[]{:S(2)}, u32[]{:S(2)}) %all-to-all-start.2) | async-done | bytes 2080 | tf_op jit(solution)/shard_map/all_to_all | solution.py:61
  258.0 2.5 gather_fusion
  (200 shorter events, 88.2 us)
Async XLA Ops:
  6.5 123.3 %all-gather.3.cloned.1.call-start = ((), (), s32[]{:S(2)}) async-start(), calls=%async_computation.3 | async-start | bytes 25952256 | tf_op jit(solution)/shard_map/all_gather | solution.py:43
  43.2 14.1 %all-to-all-start = ((s32[128,4,1]{1,2,0:T(1,128)}), s32[128,4,1]{1,2,0:T(1,128)S(1)}, u32[]{:S(2)}, u32[]{:S(2)}) async-start(s32[128,4,1]{1,2,0:T(1,128)} %bitcast.3), calls=%async_computation | async-start | bytes 131072 | tf_op jit(solution)/shard_map/all_to_all | solution.py:40
  239.7 16.9 %all-to-all-start.2 = ((f32[128,4,1]{1,2,0:T(1,128)}), f32[128,4,1]{1,2,0:T(1,128)S(1)}, u32[]{:S(2)}, u32[]{:S(2)}) async-start(f32[128,4,1]{1,2,0:T(1,128)} %bitcast.5), calls=%async_computation.2 | async-start | bytes 131072 | tf_op jit(solution)/shard_map/all_to_all | solution.py:61
Sparse Core Ops, SparseCore 0:
  41.0 88.7 all-gather.2
where the time goes:
time: 269 us; the launch traced here: 267 us
  matrix products  67.3 us (25%)
  waiting for transfers between devices  67.2 us (25%)
  blocking collectives  50.9 us (19%)
  local copies, waits for them, and re-layouts  28.4 us (11%)
  other arithmetic  26.9 us (10%)
  between operations  13.5 us (5%)
  starting transfers between devices  11.7 us (4%)
    dot_general x32, matrix products, compare(): lax.dot_general(row_emb, col_emb, (((1,), (1,)), ((), ())), preferred_ele...  67.3 us
    all_gather x1, waiting for transfers between devices, body(): piece_rows = lax.all_gather(own_rows, 'blk', axis=0, tiled=True)  48 us
    all_to_all x1, blocking collectives, body(): lax.all_to_all(send_rows, ('grp', 'blk'), split_axis=0, concat_axis=0, ti...  27.8 us
    all_gather x1, blocking collectives, body(): piece_ids = lax.all_gather(own_ids, 'blk', axis=0, tiled=True)  23 us
    dynamic_slice x64, local copies, waits for them, and re-layouts, body(): lax.scan(one_block, jnp.full((slot_count,), -1.0, jnp.float32), (stacked_...  20.2 us
    add x32, other arithmetic, body(): own_pos = lax.axis_index('blk') * slot_count + jnp.arange(slot_count)  19.5 us
    all_to_all x1, waiting for transfers between devices, body(): lax.all_to_all(send_ids, ('grp', 'blk'), split_axis=0, concat_axis=0, til...  9.64 us
    all_to_all x1, waiting for transfers between devices, body(): lax.all_to_all(best_next, ('grp', 'blk'), split_axis=0, concat_axis=0, ti...  9.59 us
  transfers between devices with their start and end apart: 3, of which 3 were waited for; matrix products, arithmetic and copies ran while one was open for 1% of the time, Pallas kernels for 0%

commit v1 on v0

v1 whole, which is shorter than its diff:
```python
import jax
import jax.numpy as jnp
from jax import lax
from jax.experimental import pallas as pl
from jax.experimental.pallas import tpu as pltpu
from jax.sharding import PartitionSpec as P

MESH = pl.DeviceIdType.MESH
LOWEST = -1.0
CHUNKS = 8
STOPS = (
    (0, 0, 0),
    (0, 2, 0),
    (1, 0, 2),
    (-1, 2, 0),
    (0, 0, 2),
    (1, 0, 1),
    (-1, -1, 0),
    (0, -1, 0),
    (0, 0, -1),
    (0, 1, 0),
    (-1, 0, 0),
    (1, 0, 0),
    (1, 0, -1),
)
SEND, WAIT, SEND_KEYS, WAIT_KEYS, TWIN, WAIT_TWIN, TWIN_KEYS, WAIT_TWIN_KEYS, PREPARE, COMPARE, FINISH = range(11)
TWINS = (0, 1, 3, 5, 6, 7, 8, 9, 10, 11)
PARTS = ((0, 1), (8, 0), (8, 1), (12, 0), (6, 0), (6, 1), (9, 0), (9, 1), (10, 0), (10, 1), (5, 0), (5, 1), (11, 0), (11, 1), (1, 0), (1, 1), (4, 0), (7, 0), (7, 1), (2, 0), (3, 0))
PROGRAM = (
    (TWIN_KEYS,),
    (SEND, 0, 0, 11, 0),
    (SEND, 0, 0, 10, 1),
    (SEND, 0, 0, 9, 2),
    (SEND, 0, 0, 8, 5),
    (SEND, 0, 0, 7, 3),
    (TWIN, 0),
    (WAIT_TWIN_KEYS,),
    (SEND_KEYS, 0, 11, 0),
    (SEND_KEYS, 0, 10, 1),
    (SEND_KEYS, 0, 9, 2),
    (SEND_KEYS, 0, 8, 5),
    (SEND_KEYS, 0, 7, 3),
    (PREPARE, 0),
    (WAIT_TWIN, 0),
    (COMPARE, 0, 0, 2, True, False),
    (SEND, 2, 0, 10, 1),
    (SEND, 3, 0, 8, 5),
    (SEND, 4, 0, 7, 3),
    (SEND, 1, 0, 11, 0),
    (SEND, 3, 0, 9, 2),
    (SEND, 2, 0, 7, 3),
    (SEND, 1, 0, 8, 5),
    (SEND, 5, 0, 11, 0),
    (SEND, 7, 0, 10, 1),
    (SEND, 7, 0, 9, 2),
    (WAIT, 11, 0),
    (WAIT, 10, 0),
    (WAIT, 9, 0),
    (WAIT, 8, 0),
    (WAIT, 7, 0),
    (SEND, 0, 11, 5, 4),
    (SEND, 1, 0, 7, 3),
    (SEND, 4, 0, 8, 5),
    (SEND, 4, 0, 11, 0),
    (SEND, 1, 0, 10, 1),
    (SEND, 1, 0, 9, 2),
    (WAIT, 10, 2),
    (WAIT, 8, 3),
    (WAIT, 7, 4),
    (WAIT, 11, 1),
    (WAIT, 9, 3),
    (SEND, 1, 11, 5, 4),
    (SEND, 3, 0, 7, 3),
    (SEND, 3, 0, 10, 1),
    (SEND, 2, 0, 11, 0),
    (SEND, 2, 0, 9, 2),
    (SEND, 2, 0, 8, 5),
    (WAIT, 7, 2),
    (WAIT, 8, 1),
    (WAIT, 11, 5),
    (WAIT, 10, 7),
    (WAIT, 9, 7),
    (SEND, 5, 11, 5, 4),
    (SEND, 5, 0, 7, 3),
    (SEND, 3, 0, 11, 0),
    (SEND, 6, 0, 10, 1),
    (SEND, 6, 0, 9, 2),
    (SEND, 5, 0, 8, 5),
    (WAIT, 5, 0),
    (WAIT, 7, 1),
    (WAIT, 8, 4),
    (WAIT, 11, 4),
    (WAIT, 10, 1),
    (WAIT, 9, 1),
    (SEND, 4, 11, 5, 4),
    (SEND, 7, 0, 7, 3),
    (SEND, 4, 0, 9, 2),
    (SEND, 4, 0, 10, 1),
    (SEND, 7, 0, 11, 0),
    (SEND, 6, 0, 8, 5),
    (WAIT, 5, 1),
    (WAIT, 7, 3),
    (WAIT, 10, 3),
    (WAIT, 11, 2),
    (WAIT, 9, 2),
    (WAIT, 8, 2),
    (SEND, 2, 11, 5, 4),
    (SEND, 6, 0, 7, 3),
    (SEND, 5, 0, 9, 2),
    (SEND, 6, 0, 11, 0),
    (SEND, 5, 0, 10, 1),
    (SEND, 7, 0, 8, 5),
    (WAIT, 5, 5),
    (WAIT, 7, 5),
    (WAIT, 11, 3),
    (WAIT, 10, 6),
    (WAIT, 9, 6),
    (WAIT, 8, 5),
    (SEND, 3, 11, 5, 4),
    (SEND, 0, 8, 12, 0),
    (SEND, 0, 7, 6, 1),
    (SEND, 2, 9, 1, 2),
    (SEND, 1, 11, 12, 5),
    (SEND, 1, 10, 6, 3),
    (WAIT, 5, 4),
    (WAIT, 7, 7),
    (WAIT, 9, 4),
    (WAIT, 10, 4),
    (WAIT, 11, 7),
    (WAIT, 8, 6),
    (SEND, 7, 11, 5, 4),
    (SEND, 1, 8, 4, 5),
    (SEND, 3, 7, 6, 1),
    (SEND, 0, 7, 1, 3),
    (SEND, 3, 9, 1, 2),
    (SEND, 2, 8, 12, 0),
    (WAIT, 5, 2),
    (WAIT, 7, 6),
    (TWIN, 7),
    (WAIT_KEYS, 7),
    (SEND_KEYS, 7, 6, 1),
    (SEND_KEYS, 7, 1, 3),
    (WAIT, 9, 5),
    (TWIN, 9),
    (WAIT_KEYS, 9),
    (WAIT, 11, 6),
    (TWIN, 11),
    (WAIT_KEYS, 11),
    (SEND_KEYS, 11, 5, 4),
    (WAIT, 10, 5),
    (TWIN, 10),
    (WAIT_KEYS, 10),
    (WAIT, 8, 7),
    (TWIN, 8),
    (WAIT_KEYS, 8),
    (SEND_KEYS, 8, 12, 0),
    (SEND_KEYS, 8, 4, 5),
    (SEND, 6, 11, 5, 4),
    (SEND, 0, 8, 4, 5),
    (SEND, 2, 10, 6, 3),
    (SEND, 1, 9, 1, 2),
    (SEND, 5, 7, 6, 1),
    (SEND, 6, 8, 12, 0),
    (PREPARE, 7),
    (COMPARE, 7, 0, 0, True, True),
    (PREPARE, 8),
    (COMPARE, 8, 0, 0, True, False),
    (WAIT, 5, 3),
    (WAIT, 12, 0),
    (WAIT, 6, 0),
    (WAIT, 1, 2),
    (WAIT, 12, 1),
    (WAIT, 6, 1),
    (SEND, 1, 5, 2, 4),
    (SEND, 3, 8, 4, 5),
    (SEND, 4, 7, 1, 3),
    (SEND, 6, 9, 1, 2),
    (SEND, 3, 8, 12, 0),
    (SEND, 6, 7, 6, 1),
    (PREPARE, 10),
    (COMPARE, 10, 0, 0, True, False),
    (FINISH, 0, True, True),
    (WAIT_TWIN, 8),
    (COMPARE, 7, 8, 0, False, True),
    (WAIT, 5, 7),
    (WAIT, 4, 1),
    (WAIT, 6, 3),
    (WAIT, 1, 0),
    (WAIT, 1, 3),
    (WAIT, 12, 2),
    (SEND, 2, 5, 2, 4),
    (SEND, 6, 8, 4, 5),
    (SEND, 7, 10, 6, 3),
    (SEND, 7, 9, 1, 2),
    (SEND, 7, 8, 12, 0),
    (SEND, 4, 7, 6, 1),
    (WAIT_TWIN, 9),
    (COMPARE, 7, 9, 1, False, False),
    (WAIT_TWIN, 10),
    (COMPARE, 7, 10, 0, False, True),
    (WAIT, 5, 6),
    (TWIN, 5),
    (WAIT_KEYS, 5),
    (SEND_KEYS, 5, 2, 4),
    (WAIT, 4, 0),
    (WAIT, 6, 2),
    (WAIT, 1, 1),
    (WAIT, 6, 5),
    (WAIT, 12, 6),
    (SEND, 0, 5, 2, 4),
    (SEND, 4, 8, 4, 5),
    (SEND, 5, 9, 1, 2),
    (SEND, 5, 8, 12, 0),
    (SEND, 1, 1, 3, 1),
    (SEND, 2, 6, 3, 3),
    (WAIT_TWIN, 11),
    (COMPARE, 7, 11, 0, False, True),
    (COMPARE, 8, 9, 0, False, True),
    (WAIT, 2, 1),
    (WAIT, 4, 3),
    (WAIT, 1, 4),
    (WAIT, 1, 6),
    (WAIT, 12, 3),
    (WAIT, 6, 6),
    (SEND, 5, 5, 2, 4),
    (SEND, 2, 8, 4, 5),
    (SEND, 4, 8, 12, 0),
    (SEND, 0, 6, 3, 3),
    (SEND, 3, 1, 3, 1),
    (COMPARE, 8, 10, 0, False, False),
    (COMPARE, 8, 11, 0, False, False),
    (WAIT, 2, 2),
    (COMPARE, 10, 11, 1, False, False),
    (WAIT, 4, 6),
    (WAIT, 6, 7),
    (WAIT, 1, 7),
    (WAIT, 12, 7),
    (WAIT, 6, 4),
    (TWIN, 6),
    (WAIT_KEYS, 6),
    (SEND_KEYS, 6, 3, 3),
    (SEND, 4, 5, 2, 4),
    (SEND, 5, 8, 4, 5),
    (SEND, 4, 6, 3, 3),
    (SEND, 3, 4, 2, 0),
    (SEND, 6, 1, 3, 1),
    (PREPARE, 5),
    (WAIT_TWIN, 7),
    (COMPARE, 5, 7, 0, True, True),
    (WAIT, 2, 0),
    (COMPARE, 5, 8, 0, False, False),
    (WAIT, 4, 4),
    (WAIT, 1, 5),
    (TWIN, 1),
    (WAIT_KEYS, 1),
    (WAIT, 12, 5),
    (WAIT, 3, 1),
    (WAIT, 3, 2),
    (SEND, 7, 5, 2, 4),
    (SEND, 7, 8, 4, 5),
    (SEND, 5, 6, 3, 3),
    (SEND, 6, 4, 2, 0),
    (SEND, 7, 1, 3, 1),
    (COMPARE, 5, 9, 0, False, False),
    (COMPARE, 5, 10, 0, False, False),
    (WAIT, 2, 5),
    (WAIT, 4, 2),
    (WAIT, 12, 4),
    (WAIT_KEYS, 12),
    (WAIT, 3, 0),
    (WAIT, 3, 3),
    (PREPARE, 6),
    (WAIT_TWIN, 5),
    (COMPARE, 6, 5, 0, True, True),
    (COMPARE, 6, 8, 0, False, False),
    (COMPARE, 6, 9, 0, False, False),
    (WAIT, 2, 4),
    (COMPARE, 6, 11, 0, False, False),
    (WAIT, 4, 5),
    (WAIT, 3, 4),
    (WAIT, 2, 3),
    (WAIT, 3, 6),
    (PREPARE, 1),
    (COMPARE, 1, 5, 0, True, False),
    (COMPARE, 1, 8, 0, False, False),
    (FINISH, 8, True, True),
    (PREPARE, 12),
    (WAIT_TWIN, 1),
    (COMPARE, 12, 1, 0, True, True),
    (WAIT, 2, 7),
    (WAIT, 4, 7),
    (WAIT_KEYS, 4),
    (WAIT, 3, 5),
    (WAIT, 2, 6),
    (WAIT_KEYS, 2),
    (WAIT, 3, 7),
    (TWIN, 3),
    (WAIT_KEYS, 3),
    (COMPARE, 12, 5, 1, False, False),
    (WAIT_TWIN, 6),
    (COMPARE, 12, 6, 0, False, True),
    (COMPARE, 12, 9, 0, False, False),
    (FINISH, 12, True, False),
    (PREPARE, 2),
    (COMPARE, 2, 1, 0, True, False),
    (COMPARE, 2, 6, 0, False, False),
    (FINISH, 6, True, True),
    (COMPARE, 2, 7, 0, False, False),
    (COMPARE, 2, 9, 0, False, False),
    (FINISH, 9, False, True),
    (COMPARE, 2, 10, 1, False, False),
    (FINISH, 10, True, True),
    (PREPARE, 3),
    (COMPARE, 3, 5, 0, True, False),
    (FINISH, 5, True, True),
    (COMPARE, 3, 11, 1, False, False),
    (FINISH, 11, False, True),
    (PREPARE, 4),
    (COMPARE, 4, 1, 1, True, False),
    (FINISH, 1, True, True),
    (COMPARE, 4, 7, 0, False, False),
    (FINISH, 4, True, False),
    (FINISH, 7, True, True),
    (WAIT_TWIN, 3),
    (COMPARE, 2, 3, 1, False, False),
    (FINISH, 2, True, False),
    (FINISH, 3, True, False),
)
STEPS_IN = ((1, 0, 0), (-1, 0, 0), (0, 1, 0), (0, -1, 0), (0, 0, 1), (0, 0, -1))
COUNT = len(STOPS)


def at_offset(offset, other_core):
    z, blk = lax.axis_index("grp"), lax.axis_index("blk")
    core, x, y = blk % 2, blk // 2 % 4, blk // 8
    if other_core:
        core = 1 - core
    x, y, z = (x + offset[0] + 4) % 4, (y + offset[1] + 4) % 4, (z + offset[2] + 4) % 4
    return (z, (y * 4 + x) * 2 + core)


def kernel(
    x_ref, target_ref, cluster_ref, out_ref,
    rows, keys, key_cols, row_max, col_max, parts, heard,
    row_sent, row_got, key_sent, key_got, twin_sent, twin_got, twin_key, part_sent, part_got,
):
    size, width = x_ref.shape
    piece = size // CHUNKS
    here = (0, 0, 0)
    barrier = pltpu.get_barrier_semaphore()
    near = [at_offset(step, False) for step in STEPS_IN] + [at_offset(here, True)]
    for device in near:
        pl.semaphore_signal(barrier, inc=1, device_id=device, device_id_type=MESH)

    key = jnp.right_shift(target_ref[...], 5) * 64 + cluster_ref[...]
    keys[0, 0] = key.astype(jnp.float32)

    def normalize(part):
        here_rows = pl.ds(part * piece, piece)
        wide = x_ref[here_rows].astype(jnp.float32)
        scale_inv = lax.rsqrt(jnp.sum(wide * wide, axis=1, keepdims=True) + 1e-06)
        rows[0, 0, here_rows] = (wide * scale_inv).astype(jnp.bfloat16)

    for part in range(CHUNKS):
        normalize(part)
    pl.semaphore_wait(barrier, len(near))

    def remote(src, dst, sent, got, device):
        return pltpu.make_async_remote_copy(
            src_ref=src, dst_ref=dst, send_sem=sent, recv_sem=got, device_id=device, device_id_type=MESH
        )

    def send_rows(part, src, dst, step):
        here_rows = pl.ds(part * piece, piece)
        return remote(
            rows.at[src, 0, here_rows], rows.at[dst, 0, here_rows],
            row_sent.at[dst], row_got.at[dst, part], at_offset(STEPS_IN[step], False),
        )

    def send_keys(src, dst, step):
        return remote(
            keys.at[src], keys.at[dst], key_sent.at[dst], key_got.at[dst], at_offset(STEPS_IN[step], False)
        )

    def to_twin(slot):
        return remote(
            rows.at[slot, 0], rows.at[slot, 1], twin_sent.at[slot], twin_got.at[slot], at_offset(here, True)
        )

    def keys_to_twin():
        return remote(
            keys.at[0, 0], keys.at[0, 1], twin_key.at[0], twin_key.at[1], at_offset(here, True)
        )

    def send_part(slot, half):
        offset = tuple(-v for v in STOPS[slot])
        return remote(
            parts.at[slot, half], heard.at[slot, half],
            part_sent.at[slot, half], part_got.at[slot, half], at_offset(offset, half == 1),
        )

    def prepare(slot):
        spread = jnp.broadcast_to(keys[slot, 0], (128, size))
        key_cols[slot] = spread.T

    def compare(left, right, mode, fresh_row, fresh_col):
        best_row = None
        for half in range(2):
            scores = lax.dot_general(
                rows[left, 0], rows[right, half], (((1,), (1,)), ((), ())), preferred_element_type=jnp.float32
            )
            allowed = []
            for lane in range(0, size, 128):
                same = key_cols[left] == keys[right, half][:, lane : lane + 128]
                if mode == 2 and half == 0:
                    row_at = lax.broadcasted_iota(jnp.int32, (size, 128), 0)
                    col_at = lax.broadcasted_iota(jnp.int32, (size, 128), 1) + lane
                    same = same & (row_at != col_at)
                block = jnp.where(same, scores[:, lane : lane + 128], LOWEST)
                best_row = block if best_row is None else jnp.maximum(best_row, block)
                if mode == 0:
                    best = jnp.max(block.reshape(size // 8, 8, 128), axis=0)
                    place = (right, half, slice(None), slice(lane, lane + 128))
                    col_max[place] = best if fresh_col else jnp.maximum(col_max[place], best)
        row_max[left] = best_row if fresh_row else jnp.maximum(row_max[left], best_row)

    def finish(slot, has_row, has_col):
        best = None
        if has_row:
            best = jnp.max(row_max[slot].T, axis=0, keepdims=True)
        if has_col:
            col = jnp.max(col_max[slot, 0], axis=0, keepdims=True)
            best = col if best is None else jnp.maximum(best, col)
            parts[slot, 1] = jnp.max(col_max[slot, 1], axis=0, keepdims=True)
        parts[slot, 0] = best
        if slot or has_col:
            for half in range(2):
                if (slot or half) and (half == 0 or has_col):
                    send_part(slot, half).start()

    started = []
    for op, *args in PROGRAM:
        if op == SEND:
            send_rows(*args).start()
        elif op == WAIT:
            slot, part = args
            send_rows(part, 0, slot, 0).wait_recv()
        elif op == SEND_KEYS:
            send_keys(*args).start()
        elif op == WAIT_KEYS:
            send_keys(0, args[0], 0).wait_recv()
        elif op == TWIN:
            to_twin(args[0]).start()
        elif op == WAIT_TWIN:
            to_twin(args[0]).wait_recv()
        elif op == TWIN_KEYS:
            keys_to_twin().start()
        elif op == WAIT_TWIN_KEYS:
            keys_to_twin().wait_recv()
        elif op == PREPARE:
            prepare(*args)
        elif op == COMPARE:
            compare(*args)
        elif op == FINISH:
            finish(*args)

    for slot in range(1, COUNT):
        remote(rows.at[0, 0], rows.at[slot, 0], row_sent.at[slot], row_got.at[slot, 0], near[0]).wait_send()
        send_keys(0, slot, 0).wait_send()
    for slot in TWINS:
        to_twin(slot).wait_send()
    keys_to_twin().wait_send()
    best = parts[0, 0]
    for slot, half in PARTS:
        send_part(slot, half).wait_recv()
        best = jnp.maximum(best, heard[slot, half])
    for slot, half in PARTS:
        send_part(slot, half).wait_send()
    out_ref[...] = best


def body(embeddings, target, cluster):
    size, width = embeddings.shape
    vmem = pl.BlockSpec(memory_space=pltpu.VMEM)
    dma = pltpu.SemaphoreType.DMA
    best = pl.pallas_call(
        kernel,
        out_shape=jax.ShapeDtypeStruct((1, size), jnp.float32),
        in_specs=[vmem] * 3,
        out_specs=vmem,
        scratch_shapes=[
            pltpu.VMEM((COUNT, 2, size, width), jnp.bfloat16),
            pltpu.VMEM((COUNT, 2, 1, size), jnp.float32),
            pltpu.VMEM((COUNT, size, 128), jnp.float32),
            pltpu.VMEM((COUNT, size, 128), jnp.float32),
            pltpu.VMEM((COUNT, 2, 8, size), jnp.float32),
            pltpu.VMEM((COUNT, 2, 1, size), jnp.float32),
            pltpu.VMEM((COUNT, 2, 1, size), jnp.float32),
            dma((COUNT,)), dma((COUNT, CHUNKS)), dma((COUNT,)), dma((COUNT,)), dma((COUNT,)), dma((COUNT,)),
            dma((2,)), dma((COUNT, 2)), dma((COUNT, 2)),
        ],
        compiler_params=pltpu.CompilerParams(
            collective_id=0, has_side_effects=True, vmem_limit_bytes=48 * 2**20
        ),
        name="nearest",
    )(embeddings, target.reshape(1, size), cluster.reshape(1, size))
    return best.reshape(size)


def solution(mesh):
    return jax.shard_map(
        body,
        mesh=mesh,
        in_specs=(P(("grp", "blk"), None), P(("grp", "blk"), None), P(("grp", "blk"))),
        out_specs=P(("grp", "blk")),
        check_vma=False,
    )
```

time: 269 us -> 45.7 us (0.17)
  matrix products: 67.3 us -> 0 us
  waiting for transfers between devices: 67.2 us -> 0 us
  blocking collectives: 50.9 us -> 0 us
  Pallas kernels: 0 us -> 43.3 us
  other arithmetic: 26.9 us -> 0 us
  local copies, waits for them, and re-layouts: 28.4 us -> 2.25 us
  between operations: 13.5 us -> 0.01 us
  starting transfers between devices: 11.7 us -> 0 us
    dot_general x32 -> x0, matrix products: 67.3 us -> none  [compare(): lax.dot_general(row_emb, col_emb, (((1,), (1,)), ((), ())), preferred_ele...]
    all_gather x1 -> x0, waiting for transfers between devices: 48 us -> none  [body(): piece_rows = lax.all_gather(own_rows, 'blk', axis=0, tiled=True)]
    pallas_call x0 -> x1, Pallas kernels: none -> 43.3 us  [body(): pl.pallas_call(kernel, out_shape=jax.ShapeDtypeStruct((1, size), jnp.floa...]
    all_to_all x1 -> x0, blocking collectives: 27.8 us -> none  [body(): lax.all_to_all(send_rows, ('grp', 'blk'), split_axis=0, concat_axis=0, ti...]
    all_gather x1 -> x0, blocking collectives: 23 us -> none  [body(): piece_ids = lax.all_gather(own_ids, 'blk', axis=0, tiled=True)]
    dynamic_slice x64 -> x0, local copies, waits for them, and re-layouts: 20.2 us -> none  [body(): lax.scan(one_block, jnp.full((slot_count,), -1.0, jnp.float32), (stacked_...]
    add x32 -> x0, other arithmetic: 19.5 us -> none  [body(): own_pos = lax.axis_index('blk') * slot_count + jnp.arange(slot_count)]
    all_to_all x2 -> x0, waiting for transfers between devices: 19.2 us -> none  [the longest x1 9.64 us: body(): lax.all_to_all(send_ids, ('grp', 'blk'), split_axis=0, concat_axis=0, til...]
  transfers between devices with their start and end apart: 3 -> 0, of which waited for: 3 -> 0; matrix products, arithmetic and copies ran while one was open for 1% -> 0% of each run, Pallas kernels for 0% -> 0%
where the time goes in v1:
time: 45.7 us; the launch traced here: 45.5 us
  Pallas kernels  43.3 us (95%)
  local copies, waits for them, and re-layouts  2.25 us (5%)
    pallas_call x1, Pallas kernels, body(): pl.pallas_call(kernel, out_shape=jax.ShapeDtypeStruct((1, size), jnp.floa...  43.3 us
    unnamed x7, local copies, waits for them, and re-layouts  2.25 us

profile of v1, /device:TPU:1, one launch (start us, length us, event | category | flops | bytes accessed | tf_op | source)
XLA Modules:
  0.0 45.5 jit_solution(3153685324930084337)
XLA Ops:
  0.0 0.0 copy-start.2
  0.0 0.0 copy-start.1
  0.0 0.7 %copy-done.2 = s32[256]{0:T(256)S(1)} copy-done((s32[256]{0:T(256)S(1)}, s32[256]{0:T(256)}, u32[]{:S(2)}) %copy-start.2) | copy-done | bytes 1048
  0.7 0.0 copy-done.1
  0.7 0.0 copy-start
  0.7 1.0 %copy-done = bf16[256,768]{1,0:T(8,128)(2,1)S(1)} copy-done((bf16[256,768]{1,0:T(8,128)(2,1)S(1)}, bf16[256,768]{1,0:T(8,128)(2,1)}, u32[]{:S(2)}) %copy-start) | copy-done | bytes 393240
  1.7 43.3 %nearest.1 = f32[1,256]{1,0:T(1,128)S(1)} custom-call(bf16[256,768]{1,0:T(8,128)(2,1)S(1)} %copy-done, s32[1,256]{1,0:T(1,128)S(1)} %bitcast.4, s32[1,256]{1,0:T(1,128)S(1)} %bitcast.5), custom_call_target="tpu_custom_call" | custom-call | tf_op jit(solution)/shard_map/nearest/pallas_call | solution.py:486
  45.0 0.6 %copy.5 = f32[256]{0:T(256)} copy(f32[256]{0:T(256)S(1)} %bitcast.3) | data formatting | bytes 2048
Async XLA Ops:
  0.0 0.7 %copy-start.2 = (s32[256]{0:T(256)S(1)}, s32[256]{0:T(256)}, u32[]{:S(2)}) copy-start(s32[256]{0:T(256)} %param.5) | copy-start | bytes 3076
  0.0 0.7 %copy-start.1 = (s32[256,1]{0,1:T(1,128)S(1)}, s32[256,1]{0,1:T(1,128)}, u32[]{:S(2)}) copy-start(s32[256,1]{0,1:T(1,128)} %param.4) | copy-start | bytes 3076
  0.7 1.0 %copy-start = (bf16[256,768]{1,0:T(8,128)(2,1)S(1)}, bf16[256,768]{1,0:T(8,128)(2,1)}, u32[]{:S(2)}) copy-start(bf16[256,768]{1,0:T(8,128)(2,1)} %x_ref.1) | copy-start | bytes 1179652

commit v2 on v0

v2 whole, which is shorter than its diff:
```python
import jax
import jax.numpy as jnp
from jax import lax
from jax.experimental import pallas as pl
from jax.experimental.pallas import tpu as pltpu
from jax.sharding import PartitionSpec as P

MESH = pl.DeviceIdType.MESH
LOWEST = -1.0
CUTS = ((0, 64), (64, 64), (128, 128))
CHUNKS = len(CUTS)
STOPS = (
    (0, 0, 0),
    (0, 2, 0),
    (1, 0, 0),
    (0, 0, 2),
    (1, 2, 0),
    (-1, 0, -1),
    (-1, 0, 1),
    (0, 0, -1),
    (0, 1, 0),
    (-1, 0, 2),
    (1, -1, 0),
    (-1, 0, 0),
    (0, -1, 0),
)
(
    ENTER, NORMALIZE, OWN_KEYS, SEND, WAIT, SEND_KEYS, WAIT_KEYS, TWIN, WAIT_TWIN, TWIN_KEYS, WAIT_TWIN_KEYS, PREPARE, COMPARE, FINISH_ROWS, FINISH_COLS, TELL, HEAR, DRAIN, DRAIN_TWIN, DRAIN_TWIN_KEYS, DRAIN_TELL,
) = range(21)
PROGRAM = (
    (NORMALIZE, 0), (ENTER,), (SEND, 0, 0, 12, 3), (SEND, 0, 0, 7, 5), (SEND, 0, 0, 11, 1), (SEND, 0, 0, 8, 2),
    (SEND, 0, 0, 2, 0), (OWN_KEYS,), (TWIN_KEYS,), (TWIN, 0, 0), (NORMALIZE, 1), (TWIN, 0, 1), (NORMALIZE, 2),
    (TWIN, 0, 2), (WAIT_TWIN_KEYS,), (SEND_KEYS, 0, 12, 3), (SEND_KEYS, 0, 7, 5), (SEND_KEYS, 0, 11, 1),
    (SEND_KEYS, 0, 8, 2), (SEND_KEYS, 0, 2, 0), (PREPARE, 0), (WAIT_TWIN, 0), (COMPARE, 0, 0, 2, True, True),
    (FINISH_ROWS, 0), (SEND, 1, 0, 11, 1), (SEND, 1, 0, 12, 3), (SEND, 1, 0, 8, 2), (SEND, 2, 0, 2, 0),
    (SEND, 2, 0, 7, 5), (WAIT, 12, 0), (TWIN, 12, 0), (WAIT_KEYS, 12), (SEND_KEYS, 12, 10, 0), (PREPARE, 12),
    (WAIT, 7, 0), (TWIN, 7, 0), (WAIT_KEYS, 7), (SEND_KEYS, 7, 5, 1), (SEND_KEYS, 7, 3, 5), (PREPARE, 7),
    (WAIT, 11, 0), (TWIN, 11, 0), (WAIT_KEYS, 11), (SEND_KEYS, 11, 6, 4), (PREPARE, 11), (WAIT, 8, 0), (TWIN, 8, 0),
    (WAIT_KEYS, 8), (SEND_KEYS, 8, 1, 2), (PREPARE, 8), (WAIT, 2, 0), (WAIT_KEYS, 2), (PREPARE, 2),
    (SEND, 0, 11, 6, 4), (SEND, 0, 7, 5, 1), (SEND, 0, 8, 1, 2), (SEND, 2, 0, 12, 3), (WAIT, 11, 1), (TWIN, 11, 1),
    (WAIT, 12, 1), (TWIN, 12, 1), (WAIT, 8, 1), (TWIN, 8, 1), (SEND, 1, 11, 6, 4), (SEND, 2, 0, 11, 1),
    (SEND, 0, 12, 10, 0), (SEND, 1, 11, 5, 5), (SEND, 2, 0, 8, 2), (WAIT, 6, 0), (TWIN, 6, 0), (WAIT_KEYS, 6),
    (SEND_KEYS, 6, 9, 4), (PREPARE, 6), (WAIT, 2, 2), (WAIT, 7, 2), (TWIN, 7, 2), (WAIT, 5, 0), (TWIN, 5, 0),
    (WAIT_KEYS, 5), (PREPARE, 5), (WAIT, 1, 0), (WAIT_KEYS, 1), (SEND_KEYS, 1, 4, 0), (PREPARE, 1),
    (SEND, 0, 6, 9, 4), (SEND, 0, 1, 4, 0), (SEND, 2, 7, 3, 5), (SEND, 2, 2, 10, 3), (WAIT, 6, 1), (TWIN, 6, 1),
    (WAIT, 12, 2), (TWIN, 12, 2), (WAIT, 10, 0), (TWIN, 10, 0), (WAIT_KEYS, 10), (PREPARE, 10), (WAIT, 5, 1),
    (TWIN, 5, 1), (SEND, 1, 6, 9, 4), (SEND, 1, 5, 7, 0), (SEND, 1, 8, 1, 2), (SEND, 2, 7, 5, 1),
    (COMPARE, 12, 0, 0, True, True), (FINISH_ROWS, 12), (WAIT, 9, 0), (TWIN, 9, 0), (WAIT_KEYS, 9), (PREPARE, 9),
    (WAIT, 11, 2), (TWIN, 11, 2), (WAIT, 8, 2), (TWIN, 8, 2), (WAIT, 4, 0), (TWIN, 4, 0), (WAIT_KEYS, 4),
    (PREPARE, 4), (SEND, 2, 11, 6, 4), (SEND, 0, 7, 3, 5), (SEND, 1, 12, 10, 0), (SEND, 2, 8, 1, 2),
    (COMPARE, 11, 0, 0, True, False), (WAIT_TWIN, 12), (COMPARE, 11, 12, 0, False, True),
    (COMPARE, 8, 12, 1, True, False), (FINISH_ROWS, 8), (WAIT_TWIN, 8), (COMPARE, 11, 8, 0, False, True),
    (FINISH_ROWS, 11), (WAIT, 9, 1), (TWIN, 9, 1), (WAIT, 3, 2), (TWIN, 3, 2), (WAIT, 10, 2), (TWIN, 10, 2),
    (SEND, 2, 10, 4, 3), (WAIT, 7, 1), (TWIN, 7, 1), (WAIT, 1, 1), (SEND, 1, 7, 3, 5), (SEND, 1, 1, 4, 0),
    (SEND, 2, 3, 9, 1), (COMPARE, 7, 12, 0, True, False), (COMPARE, 7, 8, 0, False, False),
    (COMPARE, 7, 0, 0, False, False), (WAIT_TWIN, 11), (COMPARE, 7, 11, 0, False, True), (FINISH_ROWS, 7),
    (WAIT, 3, 0), (TWIN, 3, 0), (WAIT_KEYS, 3), (PREPARE, 3), (WAIT, 5, 2), (TWIN, 5, 2), (WAIT, 10, 1),
    (TWIN, 10, 1), (SEND, 1, 10, 2, 2), (COMPARE, 5, 12, 0, True, False), (COMPARE, 5, 8, 0, False, False),
    (COMPARE, 5, 0, 0, False, False), (COMPARE, 10, 8, 0, True, False), (COMPARE, 10, 11, 0, False, False),
    (FINISH_ROWS, 10), (FINISH_COLS, 11, True), (TELL, 11, 0), (TELL, 11, 1), (WAIT_TWIN, 10),
    (COMPARE, 5, 10, 0, False, True), (FINISH_ROWS, 5), (WAIT, 6, 2), (TWIN, 6, 2), (WAIT, 1, 2), (WAIT, 3, 1),
    (TWIN, 3, 1), (WAIT, 4, 1), (TWIN, 4, 1), (WAIT_TWIN, 7), (COMPARE, 6, 7, 0, True, True),
    (COMPARE, 6, 10, 0, False, False), (COMPARE, 6, 12, 0, False, False), (FINISH_COLS, 12, True), (TELL, 12, 0),
    (TELL, 12, 1), (COMPARE, 6, 8, 0, False, False), (FINISH_ROWS, 6), (COMPARE, 3, 8, 0, True, False),
    (COMPARE, 3, 10, 0, False, False), (FINISH_ROWS, 3), (COMPARE, 1, 7, 0, True, False), (FINISH_COLS, 7, True),
    (TELL, 7, 0), (TELL, 7, 1), (WAIT_TWIN, 5), (COMPARE, 1, 5, 0, False, True), (FINISH_COLS, 5, True), (TELL, 5, 0),
    (TELL, 5, 1), (WAIT, 4, 2), (TWIN, 4, 2), (WAIT, 2, 1), (WAIT, 9, 2), (TWIN, 9, 2), (WAIT_TWIN, 6),
    (COMPARE, 4, 6, 0, True, True), (COMPARE, 4, 11, 1, False, False), (WAIT_TWIN, 3),
    (COMPARE, 4, 3, 0, False, True), (FINISH_COLS, 3, True), (TELL, 3, 0), (TELL, 3, 1), (FINISH_ROWS, 4),
    (TELL, 4, 0), (COMPARE, 9, 8, 0, True, False), (FINISH_COLS, 8, True), (TELL, 8, 0), (TELL, 8, 1),
    (COMPARE, 9, 10, 0, False, False), (FINISH_COLS, 10, True), (TELL, 10, 0), (TELL, 10, 1), (WAIT_TWIN, 4),
    (COMPARE, 9, 4, 1, False, True), (FINISH_ROWS, 9), (TELL, 9, 0), (COMPARE, 1, 6, 0, False, False),
    (COMPARE, 1, 3, 1, False, False), (FINISH_ROWS, 1), (TELL, 1, 0), (COMPARE, 2, 6, 0, True, False),
    (FINISH_COLS, 6, True), (TELL, 6, 0), (TELL, 6, 1), (COMPARE, 2, 11, 1, False, False), (WAIT_TWIN, 9),
    (COMPARE, 2, 9, 1, False, True), (FINISH_ROWS, 2), (TELL, 2, 0), (COMPARE, 3, 0, 3, False, False),
    (FINISH_COLS, 0, True), (TELL, 0, 1), (DRAIN, 1), (DRAIN, 2), (DRAIN, 3), (DRAIN, 4), (DRAIN, 5), (DRAIN, 6),
    (DRAIN, 7), (DRAIN, 8), (DRAIN, 9), (DRAIN, 10), (DRAIN, 11), (DRAIN, 12), (DRAIN_TWIN, 0), (DRAIN_TWIN, 3),
    (DRAIN_TWIN, 4), (DRAIN_TWIN, 5), (DRAIN_TWIN, 6), (DRAIN_TWIN, 7), (DRAIN_TWIN, 8), (DRAIN_TWIN, 9),
    (DRAIN_TWIN, 10), (DRAIN_TWIN, 11), (DRAIN_TWIN, 12), (DRAIN_TWIN_KEYS,), (HEAR, 11, 0), (HEAR, 11, 1),
    (HEAR, 12, 0), (HEAR, 12, 1), (HEAR, 7, 0), (HEAR, 7, 1), (HEAR, 5, 0), (HEAR, 5, 1), (HEAR, 3, 0), (HEAR, 3, 1),
    (HEAR, 4, 0), (HEAR, 8, 0), (HEAR, 8, 1), (HEAR, 10, 0), (HEAR, 10, 1), (HEAR, 9, 0), (HEAR, 1, 0), (HEAR, 6, 0),
    (HEAR, 6, 1), (HEAR, 2, 0), (HEAR, 0, 1), (DRAIN_TELL, 11, 0), (DRAIN_TELL, 11, 1), (DRAIN_TELL, 12, 0),
    (DRAIN_TELL, 12, 1), (DRAIN_TELL, 7, 0), (DRAIN_TELL, 7, 1), (DRAIN_TELL, 5, 0), (DRAIN_TELL, 5, 1),
    (DRAIN_TELL, 3, 0), (DRAIN_TELL, 3, 1), (DRAIN_TELL, 4, 0), (DRAIN_TELL, 8, 0), (DRAIN_TELL, 8, 1),
    (DRAIN_TELL, 10, 0), (DRAIN_TELL, 10, 1), (DRAIN_TELL, 9, 0), (DRAIN_TELL, 1, 0), (DRAIN_TELL, 6, 0),
    (DRAIN_TELL, 6, 1), (DRAIN_TELL, 2, 0), (DRAIN_TELL, 0, 1),
)
BOTH, ROWS, OWN, COLS = range(4)
STEPS_IN = ((1, 0, 0), (-1, 0, 0), (0, 1, 0), (0, -1, 0), (0, 0, 1), (0, 0, -1))
COUNT = len(STOPS)


def at_offset(offset, other_core):
    z, blk = lax.axis_index("grp"), lax.axis_index("blk")
    core, x, y = blk % 2, blk // 2 % 4, blk // 8
    if other_core:
        core = 1 - core
    x, y, z = (x + offset[0] + 4) % 4, (y + offset[1] + 4) % 4, (z + offset[2] + 4) % 4
    return (z, (y * 4 + x) * 2 + core)


def kernel(
    x_hbm, target_hbm, cluster_hbm, out_ref,
    raw, target, cluster, rows, keys, key_cols, row_max, col_max, parts, heard,
    copied, row_sent, row_got, key_sent, key_got, twin_sent, twin_got, twin_key, part_sent, part_got,
):
    size = raw.shape[0]
    here = (0, 0, 0)
    def piece(part):
        return pl.ds(CUTS[part][0], CUTS[part][1])

    def load(part):
        return pltpu.make_async_copy(x_hbm.at[piece(part)], raw.at[piece(part)], copied.at[part])

    load_target = pltpu.make_async_copy(target_hbm, target, copied.at[CHUNKS])
    load_cluster = pltpu.make_async_copy(cluster_hbm, cluster, copied.at[CHUNKS + 1])
    for part in range(CHUNKS):
        load(part).start()
    load_target.start()
    load_cluster.start()

    barrier = pltpu.get_barrier_semaphore()
    near = [at_offset(step, False) for step in STEPS_IN] + [at_offset(here, True)]
    for device in near:
        pl.semaphore_signal(barrier, inc=1, device_id=device, device_id_type=MESH)

    def normalize(part):
        load(part).wait()
        wide = raw[piece(part)].astype(jnp.float32)
        scale_inv = lax.rsqrt(jnp.sum(wide * wide, axis=1, keepdims=True) + 1e-06)
        rows[0, 0, piece(part)] = (wide * scale_inv).astype(jnp.bfloat16)

    def own_keys():
        load_target.wait()
        load_cluster.wait()
        key = jnp.right_shift(target[...], 5) * 64 + cluster[...]
        keys[0, 0] = key.astype(jnp.float32)

    def remote(src, dst, sent, got, device):
        return pltpu.make_async_remote_copy(
            src_ref=src, dst_ref=dst, send_sem=sent, recv_sem=got, device_id=device, device_id_type=MESH
        )

    def send_rows(part, src, dst, step):
        return remote(
            rows.at[src, 0, piece(part)], rows.at[dst, 0, piece(part)],
            row_sent.at[dst], row_got.at[dst, part], near[step],
        )

    def send_keys(src, dst, step):
        return remote(keys.at[src], keys.at[dst], key_sent.at[dst], key_got.at[dst], near[step])

    def to_twin(slot, where):
        return remote(rows.at[slot, 0, where], rows.at[slot, 1, where], twin_sent.at[slot], twin_got.at[slot], near[6])

    def keys_to_twin():
        return remote(keys.at[0, 0], keys.at[0, 1], twin_key.at[0], twin_key.at[1], near[6])

    def send_part(slot, half):
        offset = tuple(-v for v in STOPS[slot])
        return remote(
            parts.at[slot, half], heard.at[slot, half],
            part_sent.at[slot, half], part_got.at[slot, half], at_offset(offset, half == 1),
        )

    def prepare(slot):
        spread = jnp.broadcast_to(keys[slot, 0], (128, size))
        key_cols[slot] = spread.T

    def compare(left, right, mode, fresh_row, fresh_col):
        best_row = None
        for half in range(2):
            scores = lax.dot_general(
                rows[left, 0], rows[right, half], (((1,), (1,)), ((), ())), preferred_element_type=jnp.float32
            )
            for lane in range(0, size, 128):
                same = key_cols[left] == keys[right, half][:, lane : lane + 128]
                if mode == OWN and half == 0:
                    row_at = lax.broadcasted_iota(jnp.int32, (size, 128), 0)
                    col_at = lax.broadcasted_iota(jnp.int32, (size, 128), 1) + lane
                    same = same & (row_at != col_at)
                block = jnp.where(same, scores[:, lane : lane + 128], LOWEST)
                if mode != COLS:
                    best_row = block if best_row is None else jnp.maximum(best_row, block)
                if mode in (BOTH, COLS):
                    best = jnp.max(block.reshape(size // 8, 8, 128), axis=0)
                    place = (right, half, slice(None), slice(lane, lane + 128))
                    col_max[place] = best if fresh_col else jnp.maximum(col_max[place], best)
        if mode != COLS:
            row_max[left] = best_row if fresh_row else jnp.maximum(row_max[left], best_row)

    def finish_rows(slot):
        parts[slot, 0] = jnp.max(row_max[slot].T, axis=0, keepdims=True)

    def finish_cols(slot, add):
        col = jnp.max(col_max[slot, 0], axis=0, keepdims=True)
        parts[slot, 0] = jnp.maximum(parts[slot, 0], col) if add else col
        parts[slot, 1] = jnp.max(col_max[slot, 1], axis=0, keepdims=True)

    def drain(slot):
        remote(rows.at[0, 0], rows.at[slot, 0], row_sent.at[slot], row_got.at[slot, 0], near[0]).wait_send()
        send_keys(0, slot, 0).wait_send()

    whole = pl.ds(0, size)

    def run(program):
        best = None
        for op, *args in program:
            if op == ENTER:
                pl.semaphore_wait(barrier, len(near))
            elif op == NORMALIZE:
                normalize(*args)
            elif op == OWN_KEYS:
                own_keys()
            elif op == SEND:
                send_rows(*args).start()
            elif op == WAIT:
                send_rows(args[1], 0, args[0], 0).wait_recv()
            elif op == SEND_KEYS:
                send_keys(*args).start()
            elif op == WAIT_KEYS:
                send_keys(0, args[0], 0).wait_recv()
            elif op == TWIN:
                to_twin(args[0], piece(args[1])).start()
            elif op == WAIT_TWIN:
                to_twin(args[0], whole).wait_recv()
            elif op == TWIN_KEYS:
                keys_to_twin().start()
            elif op == WAIT_TWIN_KEYS:
                keys_to_twin().wait_recv()
            elif op == PREPARE:
                prepare(*args)
            elif op == COMPARE:
                compare(*args)
            elif op == FINISH_ROWS:
                finish_rows(*args)
            elif op == FINISH_COLS:
                finish_cols(*args)
            elif op == TELL:
                send_part(*args).start()
            elif op == HEAR:
                send_part(*args).wait_recv()
                news = heard[args[0], args[1]]
                best = news if best is None else jnp.maximum(best, news)
            elif op == DRAIN:
                drain(*args)
            elif op == DRAIN_TWIN:
                to_twin(args[0], whole).wait_send()
            elif op == DRAIN_TWIN_KEYS:
                keys_to_twin().wait_send()
            elif op == DRAIN_TELL:
                send_part(*args).wait_send()
        out_ref[...] = jnp.maximum(best, parts[0, 0])

    run(PROGRAM)


def body(embeddings, target, cluster):
    size, width = embeddings.shape
    hbm, vmem = pl.BlockSpec(memory_space=pltpu.HBM), pl.BlockSpec(memory_space=pltpu.VMEM)
    dma = pltpu.SemaphoreType.DMA
    best = pl.pallas_call(
        kernel,
        out_shape=jax.ShapeDtypeStruct((1, size), jnp.float32),
        in_specs=[hbm] * 3,
        out_specs=vmem,
        scratch_shapes=[
            pltpu.VMEM((size, width), jnp.bfloat16),
            pltpu.VMEM((1, size), jnp.int32),
            pltpu.VMEM((1, size), jnp.int32),
            pltpu.VMEM((COUNT, 2, size, width), jnp.bfloat16),
            pltpu.VMEM((COUNT, 2, 1, size), jnp.float32),
            pltpu.VMEM((COUNT, size, 128), jnp.float32),
            pltpu.VMEM((COUNT, size, 128), jnp.float32),
            pltpu.VMEM((COUNT, 2, 8, size), jnp.float32),
            pltpu.VMEM((COUNT, 2, 1, size), jnp.float32),
            pltpu.VMEM((COUNT, 2, 1, size), jnp.float32),
            dma((CHUNKS + 2,)), dma((COUNT,)), dma((COUNT, CHUNKS)), dma((COUNT,)), dma((COUNT,)),
            dma((COUNT,)), dma((COUNT,)), dma((2,)), dma((COUNT, 2)), dma((COUNT, 2)),
        ],
        compiler_params=pltpu.CompilerParams(
            collective_id=0, has_side_effects=True, vmem_limit_bytes=56553472
        ),
        name="nearest",
    )(embeddings, target.reshape(1, size), cluster.reshape(1, size))
    return best.reshape(size)


def solution(mesh):
    return jax.shard_map(
        body,
        mesh=mesh,
        in_specs=(P(("grp", "blk"), None), P(("grp", "blk"), None), P(("grp", "blk"))),
        out_specs=P(("grp", "blk")),
        check_vma=False,
    )
```

time: 269 us -> 38.8 us (0.14)
  matrix products: 67.3 us -> 0 us
  waiting for transfers between devices: 67.2 us -> 0 us
  blocking collectives: 50.9 us -> 0 us
  Pallas kernels: 0 us -> 38.1 us
  local copies, waits for them, and re-layouts: 28.4 us -> 0.56 us
  other arithmetic: 26.9 us -> 0 us
  between operations: 13.5 us -> 0.01 us
  starting transfers between devices: 11.7 us -> 0 us
    dot_general x32 -> x0, matrix products: 67.3 us -> none  [compare(): lax.dot_general(row_emb, col_emb, (((1,), (1,)), ((), ())), preferred_ele...]
    all_gather x1 -> x0, waiting for transfers between devices: 48 us -> none  [body(): piece_rows = lax.all_gather(own_rows, 'blk', axis=0, tiled=True)]
    pallas_call x0 -> x1, Pallas kernels: none -> 38.1 us  [body(): pl.pallas_call(kernel, out_shape=jax.ShapeDtypeStruct((1, size), jnp.floa...]
    all_to_all x1 -> x0, blocking collectives: 27.8 us -> none  [body(): lax.all_to_all(send_rows, ('grp', 'blk'), split_axis=0, concat_axis=0, ti...]
    all_gather x1 -> x0, blocking collectives: 23 us -> none  [body(): piece_ids = lax.all_gather(own_ids, 'blk', axis=0, tiled=True)]
    dynamic_slice x64 -> x0, local copies, waits for them, and re-layouts: 20.2 us -> none  [body(): lax.scan(one_block, jnp.full((slot_count,), -1.0, jnp.float32), (stacked_...]
    add x32 -> x0, other arithmetic: 19.5 us -> none  [body(): own_pos = lax.axis_index('blk') * slot_count + jnp.arange(slot_count)]
    all_to_all x2 -> x0, waiting for transfers between devices: 19.2 us -> none  [the longest x1 9.64 us: body(): lax.all_to_all(send_ids, ('grp', 'blk'), split_axis=0, concat_axis=0, til...]
  transfers between devices with their start and end apart: 3 -> 0, of which waited for: 3 -> 0; matrix products, arithmetic and copies ran while one was open for 1% -> 0% of each run, Pallas kernels for 0% -> 0%
where the time goes in v2:
time: 38.8 us; the launch traced here: 38.7 us
  Pallas kernels  38.1 us (98%)
  local copies, waits for them, and re-layouts  0.56 us (1%)
    pallas_call x1, Pallas kernels, body(): pl.pallas_call(kernel, out_shape=jax.ShapeDtypeStruct((1, size), jnp.floa...  38.1 us

profile of v2, /device:TPU:1, one launch (start us, length us, event | category | flops | bytes accessed | tf_op | source)
XLA Modules:
  0.0 38.7 jit_solution(14930730335445309679)
XLA Ops:
  0.0 38.1 %nearest.1 = f32[1,256]{1,0:T(1,128)S(1)} custom-call(bf16[256,768]{1,0:T(8,128)(2,1)} %x_hbm.1, s32[1,256]{1,0:T(1,128)} %bitcast.4, s32[1,256]{1,0:T(1,128)} %bitcast.5), custom_call_target="tpu_custom_call" | custom-call | tf_op jit(solution)/shard_map/nearest/pallas_call | solution.py:262
  38.1 0.6 %copy.5 = f32[256]{0:T(256)} copy(f32[256]{0:T(256)S(1)} %bitcast.3) | data formatting | bytes 2048

commit v3 on v2

--- a/solution.py
+++ b/solution.py
@@ -7,83 +7,81 @@
 
 MESH = pl.DeviceIdType.MESH
 LOWEST = -1.0
-CUTS = ((0, 64), (64, 64), (128, 128))
+CUTS = ((0, 64), (64, 96), (160, 96))
 CHUNKS = len(CUTS)
 STOPS = (
     (0, 0, 0),
+    (0, 2, 1),
+    (2, 0, 0),
+    (0, 1, 0),
+    (-1, 0, -1),
+    (0, 0, -1),
+    (0, -1, 1),
+    (0, 0, 1),
     (0, 2, 0),
-    (1, 0, 0),
-    (0, 0, 2),
-    (1, 2, 0),
-    (-1, 0, -1),
-    (-1, 0, 1),
-    (0, 0, -1),
-    (0, 1, 0),
-    (-1, 0, 2),
-    (1, -1, 0),
     (-1, 0, 0),
+    (2, 0, -1),
     (0, -1, 0),
+    (1, 0, -1),
 )
 (
     ENTER, NORMALIZE, OWN_KEYS, SEND, WAIT, SEND_KEYS, WAIT_KEYS, TWIN, WAIT_TWIN, TWIN_KEYS, WAIT_TWIN_KEYS, PREPARE, COMPARE, FINISH_ROWS, FINISH_COLS, TELL, HEAR, DRAIN, DRAIN_TWIN, DRAIN_TWIN_KEYS, DRAIN_TELL,
 ) = range(21)
 PROGRAM = (
-    (NORMALIZE, 0), (ENTER,), (SEND, 0, 0, 12, 3), (SEND, 0, 0, 7, 5), (SEND, 0, 0, 11, 1), (SEND, 0, 0, 8, 2),
-    (SEND, 0, 0, 2, 0), (OWN_KEYS,), (TWIN_KEYS,), (TWIN, 0, 0), (NORMALIZE, 1), (TWIN, 0, 1), (NORMALIZE, 2),
-    (TWIN, 0, 2), (WAIT_TWIN_KEYS,), (SEND_KEYS, 0, 12, 3), (SEND_KEYS, 0, 7, 5), (SEND_KEYS, 0, 11, 1),
-    (SEND_KEYS, 0, 8, 2), (SEND_KEYS, 0, 2, 0), (PREPARE, 0), (WAIT_TWIN, 0), (COMPARE, 0, 0, 2, True, True),
-    (FINISH_ROWS, 0), (SEND, 1, 0, 11, 1), (SEND, 1, 0, 12, 3), (SEND, 1, 0, 8, 2), (SEND, 2, 0, 2, 0),
-    (SEND, 2, 0, 7, 5), (WAIT, 12, 0), (TWIN, 12, 0), (WAIT_KEYS, 12), (SEND_KEYS, 12, 10, 0), (PREPARE, 12),
-    (WAIT, 7, 0), (TWIN, 7, 0), (WAIT_KEYS, 7), (SEND_KEYS, 7, 5, 1), (SEND_KEYS, 7, 3, 5), (PREPARE, 7),
-    (WAIT, 11, 0), (TWIN, 11, 0), (WAIT_KEYS, 11), (SEND_KEYS, 11, 6, 4), (PREPARE, 11), (WAIT, 8, 0), (TWIN, 8, 0),
-    (WAIT_KEYS, 8), (SEND_KEYS, 8, 1, 2), (PREPARE, 8), (WAIT, 2, 0), (WAIT_KEYS, 2), (PREPARE, 2),
-    (SEND, 0, 11, 6, 4), (SEND, 0, 7, 5, 1), (SEND, 0, 8, 1, 2), (SEND, 2, 0, 12, 3), (WAIT, 11, 1), (TWIN, 11, 1),
-    (WAIT, 12, 1), (TWIN, 12, 1), (WAIT, 8, 1), (TWIN, 8, 1), (SEND, 1, 11, 6, 4), (SEND, 2, 0, 11, 1),
-    (SEND, 0, 12, 10, 0), (SEND, 1, 11, 5, 5), (SEND, 2, 0, 8, 2), (WAIT, 6, 0), (TWIN, 6, 0), (WAIT_KEYS, 6),
-    (SEND_KEYS, 6, 9, 4), (PREPARE, 6), (WAIT, 2, 2), (WAIT, 7, 2), (TWIN, 7, 2), (WAIT, 5, 0), (TWIN, 5, 0),
-    (WAIT_KEYS, 5), (PREPARE, 5), (WAIT, 1, 0), (WAIT_KEYS, 1), (SEND_KEYS, 1, 4, 0), (PREPARE, 1),
-    (SEND, 0, 6, 9, 4), (SEND, 0, 1, 4, 0), (SEND, 2, 7, 3, 5), (SEND, 2, 2, 10, 3), (WAIT, 6, 1), (TWIN, 6, 1),
-    (WAIT, 12, 2), (TWIN, 12, 2), (WAIT, 10, 0), (TWIN, 10, 0), (WAIT_KEYS, 10), (PREPARE, 10), (WAIT, 5, 1),
-    (TWIN, 5, 1), (SEND, 1, 6, 9, 4), (SEND, 1, 5, 7, 0), (SEND, 1, 8, 1, 2), (SEND, 2, 7, 5, 1),
-    (COMPARE, 12, 0, 0, True, True), (FINISH_ROWS, 12), (WAIT, 9, 0), (TWIN, 9, 0), (WAIT_KEYS, 9), (PREPARE, 9),
-    (WAIT, 11, 2), (TWIN, 11, 2), (WAIT, 8, 2), (TWIN, 8, 2), (WAIT, 4, 0), (TWIN, 4, 0), (WAIT_KEYS, 4),
-    (PREPARE, 4), (SEND, 2, 11, 6, 4), (SEND, 0, 7, 3, 5), (SEND, 1, 12, 10, 0), (SEND, 2, 8, 1, 2),
-    (COMPARE, 11, 0, 0, True, False), (WAIT_TWIN, 12), (COMPARE, 11, 12, 0, False, True),
-    (COMPARE, 8, 12, 1, True, False), (FINISH_ROWS, 8), (WAIT_TWIN, 8), (COMPARE, 11, 8, 0, False, True),
-    (FINISH_ROWS, 11), (WAIT, 9, 1), (TWIN, 9, 1), (WAIT, 3, 2), (TWIN, 3, 2), (WAIT, 10, 2), (TWIN, 10, 2),
-    (SEND, 2, 10, 4, 3), (WAIT, 7, 1), (TWIN, 7, 1), (WAIT, 1, 1), (SEND, 1, 7, 3, 5), (SEND, 1, 1, 4, 0),
-    (SEND, 2, 3, 9, 1), (COMPARE, 7, 12, 0, True, False), (COMPARE, 7, 8, 0, False, False),
-    (COMPARE, 7, 0, 0, False, False), (WAIT_TWIN, 11), (COMPARE, 7, 11, 0, False, True), (FINISH_ROWS, 7),
-    (WAIT, 3, 0), (TWIN, 3, 0), (WAIT_KEYS, 3), (PREPARE, 3), (WAIT, 5, 2), (TWIN, 5, 2), (WAIT, 10, 1),
-    (TWIN, 10, 1), (SEND, 1, 10, 2, 2), (COMPARE, 5, 12, 0, True, False), (COMPARE, 5, 8, 0, False, False),
-    (COMPARE, 5, 0, 0, False, False), (COMPARE, 10, 8, 0, True, False), (COMPARE, 10, 11, 0, False, False),
-    (FINISH_ROWS, 10), (FINISH_COLS, 11, True), (TELL, 11, 0), (TELL, 11, 1), (WAIT_TWIN, 10),
-    (COMPARE, 5, 10, 0, False, True), (FINISH_ROWS, 5), (WAIT, 6, 2), (TWIN, 6, 2), (WAIT, 1, 2), (WAIT, 3, 1),
-    (TWIN, 3, 1), (WAIT, 4, 1), (TWIN, 4, 1), (WAIT_TWIN, 7), (COMPARE, 6, 7, 0, True, True),
-    (COMPARE, 6, 10, 0, False, False), (COMPARE, 6, 12, 0, False, False), (FINISH_COLS, 12, True), (TELL, 12, 0),
-    (TELL, 12, 1), (COMPARE, 6, 8, 0, False, False), (FINISH_ROWS, 6), (COMPARE, 3, 8, 0, True, False),
-    (COMPARE, 3, 10, 0, False, False), (FINISH_ROWS, 3), (COMPARE, 1, 7, 0, True, False), (FINISH_COLS, 7, True),
-    (TELL, 7, 0), (TELL, 7, 1), (WAIT_TWIN, 5), (COMPARE, 1, 5, 0, False, True), (FINISH_COLS, 5, True), (TELL, 5, 0),
-    (TELL, 5, 1), (WAIT, 4, 2), (TWIN, 4, 2), (WAIT, 2, 1), (WAIT, 9, 2), (TWIN, 9, 2), (WAIT_TWIN, 6),
-    (COMPARE, 4, 6, 0, True, True), (COMPARE, 4, 11, 1, False, False), (WAIT_TWIN, 3),
-    (COMPARE, 4, 3, 0, False, True), (FINISH_COLS, 3, True), (TELL, 3, 0), (TELL, 3, 1), (FINISH_ROWS, 4),
-    (TELL, 4, 0), (COMPARE, 9, 8, 0, True, False), (FINISH_COLS, 8, True), (TELL, 8, 0), (TELL, 8, 1),
-    (COMPARE, 9, 10, 0, False, False), (FINISH_COLS, 10, True), (TELL, 10, 0), (TELL, 10, 1), (WAIT_TWIN, 4),
-    (COMPARE, 9, 4, 1, False, True), (FINISH_ROWS, 9), (TELL, 9, 0), (COMPARE, 1, 6, 0, False, False),
-    (COMPARE, 1, 3, 1, False, False), (FINISH_ROWS, 1), (TELL, 1, 0), (COMPARE, 2, 6, 0, True, False),
-    (FINISH_COLS, 6, True), (TELL, 6, 0), (TELL, 6, 1), (COMPARE, 2, 11, 1, False, False), (WAIT_TWIN, 9),
-    (COMPARE, 2, 9, 1, False, True), (FINISH_ROWS, 2), (TELL, 2, 0), (COMPARE, 3, 0, 3, False, False),
+    (NORMALIZE, 0), (ENTER,), (SEND, 0, 0, 11, 3), (SEND, 0, 0, 9, 1), (SEND, 0, 0, 7, 4), (SEND, 0, 0, 3, 2),
+    (SEND, 0, 0, 5, 5), (OWN_KEYS,), (TWIN_KEYS,), (TWIN, 0, 0), (NORMALIZE, 1), (TWIN, 0, 1), (NORMALIZE, 2),
+    (TWIN, 0, 2), (WAIT_TWIN_KEYS,), (SEND_KEYS, 0, 11, 3), (SEND_KEYS, 0, 9, 1), (SEND_KEYS, 0, 7, 4),
+    (SEND_KEYS, 0, 3, 2), (SEND_KEYS, 0, 5, 5), (PREPARE, 0), (WAIT_TWIN, 0), (COMPARE, 0, 0, 2, True, True),
+    (FINISH_ROWS, 0), (SEND, 2, 0, 11, 3), (SEND, 1, 0, 9, 1), (SEND, 2, 0, 5, 5), (SEND, 2, 0, 7, 4),
+    (SEND, 1, 0, 3, 2), (WAIT, 11, 0), (TWIN, 11, 0), (WAIT_KEYS, 11), (SEND_KEYS, 11, 6, 4), (PREPARE, 11),
+    (WAIT, 9, 0), (TWIN, 9, 0), (WAIT_KEYS, 9), (SEND_KEYS, 9, 2, 1), (PREPARE, 9), (WAIT, 7, 0), (WAIT_KEYS, 7),
+    (PREPARE, 7), (WAIT, 3, 0), (TWIN, 3, 0), (WAIT_KEYS, 3), (SEND_KEYS, 3, 8, 2), (PREPARE, 3), (WAIT, 5, 0),
+    (SEND, 0, 5, 12, 0), (SEND, 1, 0, 11, 3), (SEND, 2, 0, 9, 1), (SEND, 0, 11, 6, 4), (SEND, 1, 0, 5, 5),
+    (SEND, 0, 3, 8, 2), (TWIN, 5, 0), (WAIT_KEYS, 5), (SEND_KEYS, 5, 12, 0), (SEND_KEYS, 5, 4, 1), (PREPARE, 5),
+    (WAIT, 11, 2), (TWIN, 11, 2), (WAIT, 9, 1), (TWIN, 9, 1), (WAIT, 5, 2), (TWIN, 5, 2), (WAIT, 7, 2), (WAIT, 3, 1),
+    (SEND, 2, 5, 12, 0), (SEND, 2, 11, 6, 4), (SEND, 1, 3, 8, 2), (TWIN, 3, 1), (WAIT, 12, 0), (SEND, 1, 9, 2, 1),
+    (SEND, 1, 9, 4, 5), (SEND, 2, 11, 8, 3), (TWIN, 12, 0), (WAIT_KEYS, 12), (SEND_KEYS, 12, 10, 0), (PREPARE, 12),
+    (WAIT, 6, 0), (TWIN, 6, 0), (WAIT_KEYS, 6), (SEND_KEYS, 6, 1, 3), (PREPARE, 6), (WAIT, 8, 0), (TWIN, 8, 0),
+    (WAIT_KEYS, 8), (PREPARE, 8), (WAIT, 11, 1), (TWIN, 11, 1), (WAIT, 9, 2), (TWIN, 9, 2), (WAIT, 5, 1),
+    (SEND, 1, 5, 12, 0), (SEND, 1, 11, 6, 4), (SEND, 2, 0, 3, 2), (TWIN, 5, 1), (COMPARE, 9, 0, 0, True, True),
+    (FINISH_ROWS, 9), (COMPARE, 11, 0, 0, True, False), (COMPARE, 5, 0, 0, True, False), (SEND, 2, 9, 2, 1),
+    (SEND, 2, 9, 4, 5), (SEND, 0, 6, 1, 3), (WAIT_TWIN, 11), (COMPARE, 5, 11, 0, False, True), (WAIT_TWIN, 9),
+    (COMPARE, 5, 9, 0, False, True), (FINISH_ROWS, 5), (COMPARE, 11, 9, 0, False, False), (FINISH_ROWS, 11),
+    (WAIT, 12, 2), (TWIN, 12, 2), (WAIT, 6, 2), (TWIN, 6, 2), (WAIT, 8, 1), (TWIN, 8, 1), (WAIT, 2, 1), (WAIT, 4, 1),
+    (WAIT, 8, 2), (SEND, 2, 12, 10, 0), (SEND, 1, 8, 1, 4), (SEND, 2, 6, 1, 3), (TWIN, 8, 2), (WAIT_TWIN, 5),
+    (COMPARE, 8, 5, 0, True, True), (COMPARE, 8, 9, 0, False, False), (FINISH_ROWS, 8),
+    (COMPARE, 8, 0, 3, False, False), (SEND, 0, 9, 2, 1), (SEND, 1, 2, 10, 5), (WAIT, 12, 1), (TWIN, 12, 1),
+    (WAIT, 6, 1), (TWIN, 6, 1), (WAIT, 3, 2), (TWIN, 3, 2), (WAIT, 1, 0), (SEND, 1, 6, 7, 2), (TWIN, 1, 0),
+    (WAIT_KEYS, 1), (PREPARE, 1), (COMPARE, 12, 9, 0, True, False), (COMPARE, 12, 11, 0, False, False),
+    (FINISH_COLS, 11, True), (TELL, 11, 0), (TELL, 11, 1), (WAIT_TWIN, 8), (COMPARE, 12, 8, 0, False, True),
+    (FINISH_COLS, 8, True), (TELL, 8, 0), (TELL, 8, 1), (FINISH_ROWS, 12), (COMPARE, 6, 5, 0, True, False),
+    (WAIT, 2, 2), (WAIT, 4, 2), (SEND, 0, 12, 10, 0), (SEND, 0, 5, 4, 1), (COMPARE, 6, 9, 0, False, False),
+    (WAIT_TWIN, 12), (COMPARE, 6, 12, 0, False, True), (FINISH_ROWS, 6), (COMPARE, 3, 12, 0, True, False),
+    (COMPARE, 3, 5, 0, False, False), (FINISH_COLS, 5, True), (TELL, 5, 0), (TELL, 5, 1),
+    (COMPARE, 3, 9, 0, False, False), (FINISH_ROWS, 3), (WAIT, 10, 2), (TWIN, 10, 2), (WAIT, 1, 1), (TWIN, 1, 1),
+    (WAIT, 1, 2), (TWIN, 1, 2), (WAIT, 2, 0), (WAIT_KEYS, 2), (PREPARE, 2), (COMPARE, 1, 12, 0, True, False),
+    (COMPARE, 1, 5, 1, False, False), (COMPARE, 1, 9, 0, False, False), (FINISH_ROWS, 1), (FINISH_COLS, 9, True),
+    (TELL, 9, 0), (TELL, 9, 1), (COMPARE, 2, 8, 1, True, False), (WAIT, 10, 1), (TWIN, 10, 1), (WAIT_TWIN, 6),
+    (COMPARE, 2, 6, 0, False, True), (WAIT_TWIN, 1), (COMPARE, 2, 1, 0, False, True), (FINISH_COLS, 1, True),
+    (TELL, 1, 0), (TELL, 1, 1), (WAIT_TWIN, 3), (COMPARE, 2, 3, 0, False, True), (COMPARE, 2, 12, 0, False, False),
+    (FINISH_ROWS, 2), (TELL, 2, 0), (WAIT, 10, 0), (TWIN, 10, 0), (WAIT_KEYS, 10), (PREPARE, 10), (WAIT, 7, 1),
+    (WAIT, 4, 0), (WAIT_KEYS, 4), (PREPARE, 4), (COMPARE, 10, 3, 0, True, False), (COMPARE, 10, 6, 0, False, False),
+    (COMPARE, 10, 1, 1, False, False), (FINISH_ROWS, 10), (TELL, 10, 0), (COMPARE, 7, 12, 0, True, False),
+    (FINISH_COLS, 12, True), (TELL, 12, 0), (TELL, 12, 1), (COMPARE, 4, 3, 0, True, False), (FINISH_COLS, 3, True),
+    (TELL, 3, 0), (TELL, 3, 1), (COMPARE, 4, 6, 0, False, False), (FINISH_ROWS, 4), (TELL, 4, 0),
+    (FINISH_COLS, 6, True), (TELL, 6, 0), (TELL, 6, 1), (COMPARE, 7, 5, 1, False, False), (WAIT_TWIN, 10),
+    (COMPARE, 7, 10, 1, False, True), (FINISH_ROWS, 7), (TELL, 7, 0), (COMPARE, 2, 0, 3, False, False),
     (FINISH_COLS, 0, True), (TELL, 0, 1), (DRAIN, 1), (DRAIN, 2), (DRAIN, 3), (DRAIN, 4), (DRAIN, 5), (DRAIN, 6),
-    (DRAIN, 7), (DRAIN, 8), (DRAIN, 9), (DRAIN, 10), (DRAIN, 11), (DRAIN, 12), (DRAIN_TWIN, 0), (DRAIN_TWIN, 3),
-    (DRAIN_TWIN, 4), (DRAIN_TWIN, 5), (DRAIN_TWIN, 6), (DRAIN_TWIN, 7), (DRAIN_TWIN, 8), (DRAIN_TWIN, 9),
-    (DRAIN_TWIN, 10), (DRAIN_TWIN, 11), (DRAIN_TWIN, 12), (DRAIN_TWIN_KEYS,), (HEAR, 11, 0), (HEAR, 11, 1),
-    (HEAR, 12, 0), (HEAR, 12, 1), (HEAR, 7, 0), (HEAR, 7, 1), (HEAR, 5, 0), (HEAR, 5, 1), (HEAR, 3, 0), (HEAR, 3, 1),
-    (HEAR, 4, 0), (HEAR, 8, 0), (HEAR, 8, 1), (HEAR, 10, 0), (HEAR, 10, 1), (HEAR, 9, 0), (HEAR, 1, 0), (HEAR, 6, 0),
-    (HEAR, 6, 1), (HEAR, 2, 0), (HEAR, 0, 1), (DRAIN_TELL, 11, 0), (DRAIN_TELL, 11, 1), (DRAIN_TELL, 12, 0),
-    (DRAIN_TELL, 12, 1), (DRAIN_TELL, 7, 0), (DRAIN_TELL, 7, 1), (DRAIN_TELL, 5, 0), (DRAIN_TELL, 5, 1),
-    (DRAIN_TELL, 3, 0), (DRAIN_TELL, 3, 1), (DRAIN_TELL, 4, 0), (DRAIN_TELL, 8, 0), (DRAIN_TELL, 8, 1),
-    (DRAIN_TELL, 10, 0), (DRAIN_TELL, 10, 1), (DRAIN_TELL, 9, 0), (DRAIN_TELL, 1, 0), (DRAIN_TELL, 6, 0),
-    (DRAIN_TELL, 6, 1), (DRAIN_TELL, 2, 0), (DRAIN_TELL, 0, 1),
+    (DRAIN, 7), (DRAIN, 8), (DRAIN, 9), (DRAIN, 10), (DRAIN, 11), (DRAIN, 12), (DRAIN_TWIN, 0), (DRAIN_TWIN, 1),
+    (DRAIN_TWIN, 3), (DRAIN_TWIN, 5), (DRAIN_TWIN, 6), (DRAIN_TWIN, 8), (DRAIN_TWIN, 9), (DRAIN_TWIN, 10),
+    (DRAIN_TWIN, 11), (DRAIN_TWIN, 12), (DRAIN_TWIN_KEYS,), (HEAR, 11, 0), (HEAR, 11, 1), (HEAR, 8, 0), (HEAR, 8, 1),
+    (HEAR, 5, 0), (HEAR, 5, 1), (HEAR, 9, 0), (HEAR, 9, 1), (HEAR, 1, 0), (HEAR, 1, 1), (HEAR, 2, 0), (HEAR, 10, 0),
+    (HEAR, 12, 0), (HEAR, 12, 1), (HEAR, 3, 0), (HEAR, 3, 1), (HEAR, 4, 0), (HEAR, 6, 0), (HEAR, 6, 1), (HEAR, 7, 0),
+    (HEAR, 0, 1), (DRAIN_TELL, 11, 0), (DRAIN_TELL, 11, 1), (DRAIN_TELL, 8, 0), (DRAIN_TELL, 8, 1),
+    (DRAIN_TELL, 5, 0), (DRAIN_TELL, 5, 1), (DRAIN_TELL, 9, 0), (DRAIN_TELL, 9, 1), (DRAIN_TELL, 1, 0),
+    (DRAIN_TELL, 1, 1), (DRAIN_TELL, 2, 0), (DRAIN_TELL, 10, 0), (DRAIN_TELL, 12, 0), (DRAIN_TELL, 12, 1),
+    (DRAIN_TELL, 3, 0), (DRAIN_TELL, 3, 1), (DRAIN_TELL, 4, 0), (DRAIN_TELL, 6, 0), (DRAIN_TELL, 6, 1),
+    (DRAIN_TELL, 7, 0), (DRAIN_TELL, 0, 1),
 )
 BOTH, ROWS, OWN, COLS = range(4)
 STEPS_IN = ((1, 0, 0), (-1, 0, 0), (0, 1, 0), (0, -1, 0), (0, 0, 1), (0, 0, -1))

time: 38.8 us -> 38.3 us (0.987)
  Pallas kernels: 38.1 us -> 37.6 us
    pallas_call x1, Pallas kernels: 38.1 us -> 37.6 us  [body(): pl.pallas_call(kernel, out_shape=jax.ShapeDtypeStruct((1, size), jnp.floa...]
where the time goes in v3:
time: 38.3 us; the launch traced here: 38.2 us
  Pallas kernels  37.6 us (98%)
  local copies, waits for them, and re-layouts  0.56 us (1%)
    pallas_call x1, Pallas kernels, body(): pl.pallas_call(kernel, out_shape=jax.ShapeDtypeStruct((1, size), jnp.floa...  37.6 us

profile of v3, /device:TPU:1, one launch (start us, length us, event | category | flops | bytes accessed | tf_op | source)
XLA Modules:
  0.0 38.2 jit_solution(13892969865652350569)
XLA Ops:
  0.0 37.6 %nearest.1 = f32[1,256]{1,0:T(1,128)S(1)} custom-call(bf16[256,768]{1,0:T(8,128)(2,1)} %x_hbm.1, s32[1,256]{1,0:T(1,128)} %bitcast.4, s32[1,256]{1,0:T(1,128)} %bitcast.5), custom_call_target="tpu_custom_call" | custom-call | tf_op jit(solution)/shard_map/nearest/pallas_call | solution.py:260
  37.6 0.6 %copy.5 = f32[256]{0:T(256)} copy(f32[256]{0:T(256)S(1)} %bitcast.3) | data formatting | bytes 2048

commit v4 on v3

--- a/solution.py
+++ b/solution.py
@@ -7,81 +7,82 @@
 
 MESH = pl.DeviceIdType.MESH
 LOWEST = -1.0
-CUTS = ((0, 64), (64, 96), (160, 96))
+CUTS = ((0, 80), (80, 80), (160, 96))
 CHUNKS = len(CUTS)
 STOPS = (
     (0, 0, 0),
-    (0, 2, 1),
-    (2, 0, 0),
+    (1, 0, 0),
     (0, 1, 0),
-    (-1, 0, -1),
-    (0, 0, -1),
-    (0, -1, 1),
-    (0, 0, 1),
+    (1, 0, 1),
+    (-1, 2, 0),
+    (-1, -1, 0),
     (0, 2, 0),
     (-1, 0, 0),
-    (2, 0, -1),
-    (0, -1, 0),
-    (1, 0, -1),
+    (0, 0, -1),
+    (1, 0, 2),
+    (0, 0, 2),
+    (0, 0, 1),
+    (-1, 1, 0),
 )
 (
     ENTER, NORMALIZE, OWN_KEYS, SEND, WAIT, SEND_KEYS, WAIT_KEYS, TWIN, WAIT_TWIN, TWIN_KEYS, WAIT_TWIN_KEYS, PREPARE, COMPARE, FINISH_ROWS, FINISH_COLS, TELL, HEAR, DRAIN, DRAIN_TWIN, DRAIN_TWIN_KEYS, DRAIN_TELL,
 ) = range(21)
 PROGRAM = (
-    (NORMALIZE, 0), (ENTER,), (SEND, 0, 0, 11, 3), (SEND, 0, 0, 9, 1), (SEND, 0, 0, 7, 4), (SEND, 0, 0, 3, 2),
-    (SEND, 0, 0, 5, 5), (OWN_KEYS,), (TWIN_KEYS,), (TWIN, 0, 0), (NORMALIZE, 1), (TWIN, 0, 1), (NORMALIZE, 2),
-    (TWIN, 0, 2), (WAIT_TWIN_KEYS,), (SEND_KEYS, 0, 11, 3), (SEND_KEYS, 0, 9, 1), (SEND_KEYS, 0, 7, 4),
-    (SEND_KEYS, 0, 3, 2), (SEND_KEYS, 0, 5, 5), (PREPARE, 0), (WAIT_TWIN, 0), (COMPARE, 0, 0, 2, True, True),
-    (FINISH_ROWS, 0), (SEND, 2, 0, 11, 3), (SEND, 1, 0, 9, 1), (SEND, 2, 0, 5, 5), (SEND, 2, 0, 7, 4),
-    (SEND, 1, 0, 3, 2), (WAIT, 11, 0), (TWIN, 11, 0), (WAIT_KEYS, 11), (SEND_KEYS, 11, 6, 4), (PREPARE, 11),
-    (WAIT, 9, 0), (TWIN, 9, 0), (WAIT_KEYS, 9), (SEND_KEYS, 9, 2, 1), (PREPARE, 9), (WAIT, 7, 0), (WAIT_KEYS, 7),
-    (PREPARE, 7), (WAIT, 3, 0), (TWIN, 3, 0), (WAIT_KEYS, 3), (SEND_KEYS, 3, 8, 2), (PREPARE, 3), (WAIT, 5, 0),
-    (SEND, 0, 5, 12, 0), (SEND, 1, 0, 11, 3), (SEND, 2, 0, 9, 1), (SEND, 0, 11, 6, 4), (SEND, 1, 0, 5, 5),
-    (SEND, 0, 3, 8, 2), (TWIN, 5, 0), (WAIT_KEYS, 5), (SEND_KEYS, 5, 12, 0), (SEND_KEYS, 5, 4, 1), (PREPARE, 5),
-    (WAIT, 11, 2), (TWIN, 11, 2), (WAIT, 9, 1), (TWIN, 9, 1), (WAIT, 5, 2), (TWIN, 5, 2), (WAIT, 7, 2), (WAIT, 3, 1),
-    (SEND, 2, 5, 12, 0), (SEND, 2, 11, 6, 4), (SEND, 1, 3, 8, 2), (TWIN, 3, 1), (WAIT, 12, 0), (SEND, 1, 9, 2, 1),
-    (SEND, 1, 9, 4, 5), (SEND, 2, 11, 8, 3), (TWIN, 12, 0), (WAIT_KEYS, 12), (SEND_KEYS, 12, 10, 0), (PREPARE, 12),
-    (WAIT, 6, 0), (TWIN, 6, 0), (WAIT_KEYS, 6), (SEND_KEYS, 6, 1, 3), (PREPARE, 6), (WAIT, 8, 0), (TWIN, 8, 0),
-    (WAIT_KEYS, 8), (PREPARE, 8), (WAIT, 11, 1), (TWIN, 11, 1), (WAIT, 9, 2), (TWIN, 9, 2), (WAIT, 5, 1),
-    (SEND, 1, 5, 12, 0), (SEND, 1, 11, 6, 4), (SEND, 2, 0, 3, 2), (TWIN, 5, 1), (COMPARE, 9, 0, 0, True, True),
-    (FINISH_ROWS, 9), (COMPARE, 11, 0, 0, True, False), (COMPARE, 5, 0, 0, True, False), (SEND, 2, 9, 2, 1),
-    (SEND, 2, 9, 4, 5), (SEND, 0, 6, 1, 3), (WAIT_TWIN, 11), (COMPARE, 5, 11, 0, False, True), (WAIT_TWIN, 9),
-    (COMPARE, 5, 9, 0, False, True), (FINISH_ROWS, 5), (COMPARE, 11, 9, 0, False, False), (FINISH_ROWS, 11),
-    (WAIT, 12, 2), (TWIN, 12, 2), (WAIT, 6, 2), (TWIN, 6, 2), (WAIT, 8, 1), (TWIN, 8, 1), (WAIT, 2, 1), (WAIT, 4, 1),
-    (WAIT, 8, 2), (SEND, 2, 12, 10, 0), (SEND, 1, 8, 1, 4), (SEND, 2, 6, 1, 3), (TWIN, 8, 2), (WAIT_TWIN, 5),
-    (COMPARE, 8, 5, 0, True, True), (COMPARE, 8, 9, 0, False, False), (FINISH_ROWS, 8),
-    (COMPARE, 8, 0, 3, False, False), (SEND, 0, 9, 2, 1), (SEND, 1, 2, 10, 5), (WAIT, 12, 1), (TWIN, 12, 1),
-    (WAIT, 6, 1), (TWIN, 6, 1), (WAIT, 3, 2), (TWIN, 3, 2), (WAIT, 1, 0), (SEND, 1, 6, 7, 2), (TWIN, 1, 0),
-    (WAIT_KEYS, 1), (PREPARE, 1), (COMPARE, 12, 9, 0, True, False), (COMPARE, 12, 11, 0, False, False),
-    (FINISH_COLS, 11, True), (TELL, 11, 0), (TELL, 11, 1), (WAIT_TWIN, 8), (COMPARE, 12, 8, 0, False, True),
-    (FINISH_COLS, 8, True), (TELL, 8, 0), (TELL, 8, 1), (FINISH_ROWS, 12), (COMPARE, 6, 5, 0, True, False),
-    (WAIT, 2, 2), (WAIT, 4, 2), (SEND, 0, 12, 10, 0), (SEND, 0, 5, 4, 1), (COMPARE, 6, 9, 0, False, False),
-    (WAIT_TWIN, 12), (COMPARE, 6, 12, 0, False, True), (FINISH_ROWS, 6), (COMPARE, 3, 12, 0, True, False),
-    (COMPARE, 3, 5, 0, False, False), (FINISH_COLS, 5, True), (TELL, 5, 0), (TELL, 5, 1),
-    (COMPARE, 3, 9, 0, False, False), (FINISH_ROWS, 3), (WAIT, 10, 2), (TWIN, 10, 2), (WAIT, 1, 1), (TWIN, 1, 1),
-    (WAIT, 1, 2), (TWIN, 1, 2), (WAIT, 2, 0), (WAIT_KEYS, 2), (PREPARE, 2), (COMPARE, 1, 12, 0, True, False),
-    (COMPARE, 1, 5, 1, False, False), (COMPARE, 1, 9, 0, False, False), (FINISH_ROWS, 1), (FINISH_COLS, 9, True),
-    (TELL, 9, 0), (TELL, 9, 1), (COMPARE, 2, 8, 1, True, False), (WAIT, 10, 1), (TWIN, 10, 1), (WAIT_TWIN, 6),
-    (COMPARE, 2, 6, 0, False, True), (WAIT_TWIN, 1), (COMPARE, 2, 1, 0, False, True), (FINISH_COLS, 1, True),
-    (TELL, 1, 0), (TELL, 1, 1), (WAIT_TWIN, 3), (COMPARE, 2, 3, 0, False, True), (COMPARE, 2, 12, 0, False, False),
-    (FINISH_ROWS, 2), (TELL, 2, 0), (WAIT, 10, 0), (TWIN, 10, 0), (WAIT_KEYS, 10), (PREPARE, 10), (WAIT, 7, 1),
-    (WAIT, 4, 0), (WAIT_KEYS, 4), (PREPARE, 4), (COMPARE, 10, 3, 0, True, False), (COMPARE, 10, 6, 0, False, False),
-    (COMPARE, 10, 1, 1, False, False), (FINISH_ROWS, 10), (TELL, 10, 0), (COMPARE, 7, 12, 0, True, False),
-    (FINISH_COLS, 12, True), (TELL, 12, 0), (TELL, 12, 1), (COMPARE, 4, 3, 0, True, False), (FINISH_COLS, 3, True),
-    (TELL, 3, 0), (TELL, 3, 1), (COMPARE, 4, 6, 0, False, False), (FINISH_ROWS, 4), (TELL, 4, 0),
-    (FINISH_COLS, 6, True), (TELL, 6, 0), (TELL, 6, 1), (COMPARE, 7, 5, 1, False, False), (WAIT_TWIN, 10),
-    (COMPARE, 7, 10, 1, False, True), (FINISH_ROWS, 7), (TELL, 7, 0), (COMPARE, 2, 0, 3, False, False),
-    (FINISH_COLS, 0, True), (TELL, 0, 1), (DRAIN, 1), (DRAIN, 2), (DRAIN, 3), (DRAIN, 4), (DRAIN, 5), (DRAIN, 6),
-    (DRAIN, 7), (DRAIN, 8), (DRAIN, 9), (DRAIN, 10), (DRAIN, 11), (DRAIN, 12), (DRAIN_TWIN, 0), (DRAIN_TWIN, 1),
-    (DRAIN_TWIN, 3), (DRAIN_TWIN, 5), (DRAIN_TWIN, 6), (DRAIN_TWIN, 8), (DRAIN_TWIN, 9), (DRAIN_TWIN, 10),
-    (DRAIN_TWIN, 11), (DRAIN_TWIN, 12), (DRAIN_TWIN_KEYS,), (HEAR, 11, 0), (HEAR, 11, 1), (HEAR, 8, 0), (HEAR, 8, 1),
-    (HEAR, 5, 0), (HEAR, 5, 1), (HEAR, 9, 0), (HEAR, 9, 1), (HEAR, 1, 0), (HEAR, 1, 1), (HEAR, 2, 0), (HEAR, 10, 0),
-    (HEAR, 12, 0), (HEAR, 12, 1), (HEAR, 3, 0), (HEAR, 3, 1), (HEAR, 4, 0), (HEAR, 6, 0), (HEAR, 6, 1), (HEAR, 7, 0),
-    (HEAR, 0, 1), (DRAIN_TELL, 11, 0), (DRAIN_TELL, 11, 1), (DRAIN_TELL, 8, 0), (DRAIN_TELL, 8, 1),
-    (DRAIN_TELL, 5, 0), (DRAIN_TELL, 5, 1), (DRAIN_TELL, 9, 0), (DRAIN_TELL, 9, 1), (DRAIN_TELL, 1, 0),
-    (DRAIN_TELL, 1, 1), (DRAIN_TELL, 2, 0), (DRAIN_TELL, 10, 0), (DRAIN_TELL, 12, 0), (DRAIN_TELL, 12, 1),
-    (DRAIN_TELL, 3, 0), (DRAIN_TELL, 3, 1), (DRAIN_TELL, 4, 0), (DRAIN_TELL, 6, 0), (DRAIN_TELL, 6, 1),
-    (DRAIN_TELL, 7, 0), (DRAIN_TELL, 0, 1),
+    (NORMALIZE, 0), (ENTER,), (SEND, 0, 0, 2, 2), (SEND, 0, 0, 11, 4), (SEND, 0, 0, 8, 5), (SEND, 0, 0, 7, 1),
+    (SEND, 0, 0, 1, 0), (OWN_KEYS,), (TWIN_KEYS,), (TWIN, 0, 0), (NORMALIZE, 1), (TWIN, 0, 1), (NORMALIZE, 2),
+    (TWIN, 0, 2), (WAIT_TWIN_KEYS,), (SEND_KEYS, 0, 2, 2), (SEND_KEYS, 0, 11, 4), (SEND_KEYS, 0, 8, 5),
+    (SEND_KEYS, 0, 7, 1), (SEND_KEYS, 0, 1, 0), (PREPARE, 0), (WAIT_TWIN, 0), (COMPARE, 0, 0, 2, True, True),
+    (FINISH_ROWS, 0), (SEND, 1, 0, 2, 2), (SEND, 2, 0, 7, 1), (SEND, 1, 0, 11, 4), (SEND, 1, 0, 1, 0),
+    (SEND, 2, 0, 8, 5), (WAIT, 2, 0), (TWIN, 2, 0), (WAIT_KEYS, 2), (SEND_KEYS, 2, 6, 2), (PREPARE, 2), (WAIT, 11, 0),
+    (TWIN, 11, 0), (WAIT_KEYS, 11), (SEND_KEYS, 11, 3, 0), (PREPARE, 11), (WAIT, 8, 0), (TWIN, 8, 0), (WAIT_KEYS, 8),
+    (SEND_KEYS, 8, 10, 5), (PREPARE, 8), (WAIT, 7, 0), (TWIN, 7, 0), (WAIT_KEYS, 7), (SEND_KEYS, 7, 5, 3),
+    (PREPARE, 7), (WAIT, 1, 0), (SEND, 0, 7, 5, 3), (SEND, 0, 2, 6, 2), (SEND, 2, 0, 11, 4), (SEND, 0, 11, 3, 0),
+    (SEND, 1, 0, 7, 1), (SEND, 1, 0, 8, 5), (TWIN, 1, 0), (WAIT_KEYS, 1), (PREPARE, 1), (WAIT, 2, 1), (TWIN, 2, 1),
+    (WAIT, 11, 1), (TWIN, 11, 1), (WAIT, 1, 1), (TWIN, 1, 1), (WAIT, 7, 2), (TWIN, 7, 2), (WAIT, 8, 2),
+    (SEND, 2, 7, 5, 3), (SEND, 2, 0, 2, 2), (SEND, 2, 0, 1, 0), (SEND, 1, 2, 12, 1), (SEND, 1, 1, 3, 4),
+    (SEND, 2, 8, 10, 5), (TWIN, 8, 2), (WAIT, 5, 0), (TWIN, 5, 0), (WAIT_KEYS, 5), (PREPARE, 5), (WAIT, 6, 0),
+    (WAIT_KEYS, 6), (SEND_KEYS, 6, 4, 1), (PREPARE, 6), (WAIT, 3, 0), (TWIN, 3, 0), (WAIT_KEYS, 3),
+    (SEND_KEYS, 3, 9, 4), (PREPARE, 3), (WAIT, 11, 2), (TWIN, 11, 2), (WAIT, 7, 1), (TWIN, 7, 1), (WAIT, 8, 1),
+    (TWIN, 8, 1), (COMPARE, 7, 0, 0, True, True), (COMPARE, 11, 0, 3, True, False), (SEND, 1, 7, 5, 3),
+    (SEND, 0, 3, 9, 4), (SEND, 0, 6, 4, 1), (SEND, 1, 2, 6, 2), (SEND, 2, 11, 3, 0), (COMPARE, 8, 0, 3, True, False),
+    (SEND, 0, 8, 10, 5), (WAIT_TWIN, 11), (COMPARE, 8, 11, 1, True, True), (COMPARE, 7, 11, 0, False, True),
+    (FINISH_ROWS, 7), (WAIT_TWIN, 7), (COMPARE, 8, 7, 0, False, True), (FINISH_ROWS, 8), (WAIT, 5, 2), (TWIN, 5, 2),
+    (WAIT, 2, 2), (TWIN, 2, 2), (WAIT, 1, 2), (TWIN, 1, 2), (WAIT, 12, 1), (WAIT, 3, 1), (TWIN, 3, 1),
+    (COMPARE, 1, 7, 1, True, False), (COMPARE, 2, 0, 0, True, False), (WAIT, 10, 2), (SEND, 2, 5, 4, 3),
+    (SEND, 1, 12, 4, 2), (SEND, 2, 2, 12, 1), (SEND, 1, 3, 9, 4), (TWIN, 10, 2), (COMPARE, 2, 7, 0, False, False),
+    (COMPARE, 2, 11, 0, False, False), (SEND, 2, 10, 9, 0), (SEND, 1, 8, 10, 5), (WAIT_TWIN, 8),
+    (COMPARE, 2, 8, 0, False, True), (FINISH_ROWS, 2), (WAIT_TWIN, 2), (COMPARE, 1, 2, 0, False, True),
+    (FINISH_ROWS, 1), (WAIT, 5, 1), (TWIN, 5, 1), (WAIT, 9, 0), (WAIT_KEYS, 9), (PREPARE, 9), (WAIT, 4, 0),
+    (TWIN, 4, 0), (WAIT_KEYS, 4), (SEND_KEYS, 4, 12, 3), (PREPARE, 4), (WAIT, 6, 1), (COMPARE, 5, 11, 0, True, False),
+    (COMPARE, 5, 8, 0, False, False), (WAIT, 3, 2), (TWIN, 3, 2), (WAIT, 10, 0), (SEND, 2, 2, 6, 2), (TWIN, 10, 0),
+    (WAIT_KEYS, 10), (PREPARE, 10), (WAIT_TWIN, 1), (COMPARE, 5, 1, 0, False, True), (FINISH_COLS, 1, True),
+    (TELL, 1, 0), (TELL, 1, 1), (COMPARE, 5, 2, 0, False, False), (FINISH_ROWS, 5), (SEND, 0, 4, 12, 3),
+    (COMPARE, 3, 7, 0, True, False), (FINISH_COLS, 7, True), (TELL, 7, 0), (TELL, 7, 1),
+    (COMPARE, 3, 8, 0, False, False), (COMPARE, 3, 2, 0, False, False), (WAIT_TWIN, 5),
+    (COMPARE, 3, 5, 0, False, True), (FINISH_ROWS, 3), (WAIT, 4, 1), (TWIN, 4, 1), (WAIT, 9, 1), (WAIT, 4, 2),
+    (TWIN, 4, 2), (WAIT, 12, 2), (WAIT, 10, 1), (TWIN, 10, 1), (COMPARE, 4, 11, 0, True, False), (WAIT_TWIN, 3),
+    (COMPARE, 4, 3, 0, False, True), (WAIT, 9, 2), (COMPARE, 4, 8, 0, False, False), (COMPARE, 4, 1, 1, False, False),
+    (FINISH_ROWS, 4), (COMPARE, 9, 5, 0, True, False), (COMPARE, 9, 2, 0, False, False),
+    (COMPARE, 9, 7, 1, False, False), (WAIT_TWIN, 4), (COMPARE, 10, 4, 0, True, True), (FINISH_COLS, 4, True),
+    (TELL, 4, 0), (TELL, 4, 1), (COMPARE, 9, 4, 1, False, False), (FINISH_ROWS, 9), (TELL, 9, 0),
+    (COMPARE, 10, 5, 0, False, False), (FINISH_COLS, 5, True), (TELL, 5, 0), (TELL, 5, 1),
+    (COMPARE, 10, 2, 0, False, False), (FINISH_COLS, 2, True), (TELL, 2, 0), (TELL, 2, 1), (FINISH_ROWS, 10),
+    (TELL, 10, 0), (WAIT, 12, 0), (WAIT_KEYS, 12), (PREPARE, 12), (WAIT, 6, 2), (COMPARE, 12, 3, 0, True, False),
+    (FINISH_COLS, 3, True), (TELL, 3, 0), (TELL, 3, 1), (COMPARE, 12, 8, 0, False, False), (FINISH_COLS, 8, True),
+    (TELL, 8, 0), (TELL, 8, 1), (FINISH_ROWS, 12), (TELL, 12, 0), (COMPARE, 6, 11, 0, True, False),
+    (FINISH_COLS, 11, False), (TELL, 11, 0), (TELL, 11, 1), (WAIT_TWIN, 10), (COMPARE, 6, 10, 1, False, True),
+    (FINISH_ROWS, 6), (TELL, 6, 0), (COMPARE, 6, 0, 3, False, False), (FINISH_COLS, 0, True), (TELL, 0, 1),
+    (DRAIN, 1), (DRAIN, 2), (DRAIN, 3), (DRAIN, 4), (DRAIN, 5), (DRAIN, 6), (DRAIN, 7), (DRAIN, 8), (DRAIN, 9),
+    (DRAIN, 10), (DRAIN, 11), (DRAIN, 12), (DRAIN_TWIN, 0), (DRAIN_TWIN, 1), (DRAIN_TWIN, 2), (DRAIN_TWIN, 3),
+    (DRAIN_TWIN, 4), (DRAIN_TWIN, 5), (DRAIN_TWIN, 7), (DRAIN_TWIN, 8), (DRAIN_TWIN, 10), (DRAIN_TWIN, 11),
+    (DRAIN_TWIN_KEYS,), (HEAR, 1, 0), (HEAR, 1, 1), (HEAR, 7, 0), (HEAR, 7, 1), (HEAR, 4, 0), (HEAR, 4, 1),
+    (HEAR, 9, 0), (HEAR, 5, 0), (HEAR, 5, 1), (HEAR, 2, 0), (HEAR, 2, 1), (HEAR, 10, 0), (HEAR, 3, 0), (HEAR, 3, 1),
+    (HEAR, 8, 0), (HEAR, 8, 1), (HEAR, 12, 0), (HEAR, 11, 0), (HEAR, 11, 1), (HEAR, 6, 0), (HEAR, 0, 1),
+    (DRAIN_TELL, 1, 0), (DRAIN_TELL, 1, 1), (DRAIN_TELL, 7, 0), (DRAIN_TELL, 7, 1), (DRAIN_TELL, 4, 0),
+    (DRAIN_TELL, 4, 1), (DRAIN_TELL, 9, 0), (DRAIN_TELL, 5, 0), (DRAIN_TELL, 5, 1), (DRAIN_TELL, 2, 0),
+    (DRAIN_TELL, 2, 1), (DRAIN_TELL, 10, 0), (DRAIN_TELL, 3, 0), (DRAIN_TELL, 3, 1), (DRAIN_TELL, 8, 0),
+    (DRAIN_TELL, 8, 1), (DRAIN_TELL, 12, 0), (DRAIN_TELL, 11, 0), (DRAIN_TELL, 11, 1), (DRAIN_TELL, 6, 0),
+    (DRAIN_TELL, 0, 1),
 )
 BOTH, ROWS, OWN, COLS = range(4)
 STEPS_IN = ((1, 0, 0), (-1, 0, 0), (0, 1, 0), (0, -1, 0), (0, 0, 1), (0, 0, -1))

time: 38.3 us -> 37.7 us (0.984)
  Pallas kernels: 37.6 us -> 37 us
    pallas_call x1, Pallas kernels: 37.6 us -> 37 us  [body(): pl.pallas_call(kernel, out_shape=jax.ShapeDtypeStruct((1, size), jnp.floa...]
where the time goes in v4:
time: 37.7 us; the launch traced here: 37.6 us
  Pallas kernels  37 us (98%)
  local copies, waits for them, and re-layouts  0.56 us (1%)
    pallas_call x1, Pallas kernels, body(): pl.pallas_call(kernel, out_shape=jax.ShapeDtypeStruct((1, size), jnp.floa...  37 us

profile of v4, /device:TPU:1, one launch (start us, length us, event | category | flops | bytes accessed | tf_op | source)
XLA Modules:
  0.0 37.6 jit_solution(4335250119280267544)
XLA Ops:
  0.0 37.0 %nearest.1 = f32[1,256]{1,0:T(1,128)S(1)} custom-call(bf16[256,768]{1,0:T(8,128)(2,1)} %x_hbm.1, s32[1,256]{1,0:T(1,128)} %bitcast.4, s32[1,256]{1,0:T(1,128)} %bitcast.5), custom_call_target="tpu_custom_call" | custom-call | tf_op jit(solution)/shard_map/nearest/pallas_call | solution.py:261
  37.0 0.6 %copy.5 = f32[256]{0:T(256)} copy(f32[256]{0:T(256)S(1)} %bitcast.3) | data formatting | bytes 2048

commit v5 on v4

--- a/solution.py
+++ b/solution.py
@@ -105,6 +105,11 @@
 ):
     size = raw.shape[0]
     here = (0, 0, 0)
+    barrier = pltpu.get_barrier_semaphore()
+    near = [at_offset(step, False) for step in STEPS_IN] + [at_offset(here, True)]
+    for device in near:
+        pl.semaphore_signal(barrier, inc=1, device_id=device, device_id_type=MESH)
+
     def piece(part):
         return pl.ds(CUTS[part][0], CUTS[part][1])
 
@@ -117,11 +122,6 @@
         load(part).start()
     load_target.start()
     load_cluster.start()
-
-    barrier = pltpu.get_barrier_semaphore()
-    near = [at_offset(step, False) for step in STEPS_IN] + [at_offset(here, True)]
-    for device in near:
-        pl.semaphore_signal(barrier, inc=1, device_id=device, device_id_type=MESH)
 
     def normalize(part):
         load(part).wait()

time: 37.7 us -> 37.7 us (level)
  no operation moved by 1% of the time
where the time goes in v5:
time: 37.7 us; the launch traced here: 37.6 us
  Pallas kernels  37 us (98%)
  local copies, waits for them, and re-layouts  0.56 us (1%)
    pallas_call x1, Pallas kernels, body(): pl.pallas_call(kernel, out_shape=jax.ShapeDtypeStruct((1, size), jnp.floa...  37 us

profile of v5, /device:TPU:1, one launch (start us, length us, event | category | flops | bytes accessed | tf_op | source)
XLA Modules:
  0.0 37.6 jit_solution(11267135530306087741)
XLA Ops:
  0.0 37.0 %nearest.1 = f32[1,256]{1,0:T(1,128)S(1)} custom-call(bf16[256,768]{1,0:T(8,128)(2,1)} %x_hbm.1, s32[1,256]{1,0:T(1,128)} %bitcast.4, s32[1,256]{1,0:T(1,128)} %bitcast.5), custom_call_target="tpu_custom_call" | custom-call | tf_op jit(solution)/shard_map/nearest/pallas_call | solution.py:261
  37.0 0.6 %copy.5 = f32[256]{0:T(256)} copy(f32[256]{0:T(256)S(1)} %bitcast.3) | data formatting | bytes 2048

commit v6 on v4

--- a/solution.py
+++ b/solution.py
@@ -30,11 +30,11 @@
 PROGRAM = (
     (NORMALIZE, 0), (ENTER,), (SEND, 0, 0, 2, 2), (SEND, 0, 0, 11, 4), (SEND, 0, 0, 8, 5), (SEND, 0, 0, 7, 1),
     (SEND, 0, 0, 1, 0), (OWN_KEYS,), (TWIN_KEYS,), (TWIN, 0, 0), (NORMALIZE, 1), (TWIN, 0, 1), (NORMALIZE, 2),
-    (TWIN, 0, 2), (WAIT_TWIN_KEYS,), (SEND_KEYS, 0, 2, 2), (SEND_KEYS, 0, 11, 4), (SEND_KEYS, 0, 8, 5),
-    (SEND_KEYS, 0, 7, 1), (SEND_KEYS, 0, 1, 0), (PREPARE, 0), (WAIT_TWIN, 0), (COMPARE, 0, 0, 2, True, True),
-    (FINISH_ROWS, 0), (SEND, 1, 0, 2, 2), (SEND, 2, 0, 7, 1), (SEND, 1, 0, 11, 4), (SEND, 1, 0, 1, 0),
-    (SEND, 2, 0, 8, 5), (WAIT, 2, 0), (TWIN, 2, 0), (WAIT_KEYS, 2), (SEND_KEYS, 2, 6, 2), (PREPARE, 2), (WAIT, 11, 0),
-    (TWIN, 11, 0), (WAIT_KEYS, 11), (SEND_KEYS, 11, 3, 0), (PREPARE, 11), (WAIT, 8, 0), (TWIN, 8, 0), (WAIT_KEYS, 8),
+    (TWIN, 0, 2), (SEND, 1, 0, 2, 2), (SEND, 2, 0, 7, 1), (SEND, 1, 0, 11, 4), (SEND, 1, 0, 1, 0), (SEND, 2, 0, 8, 5),
+    (WAIT_TWIN_KEYS,), (SEND_KEYS, 0, 2, 2), (SEND_KEYS, 0, 11, 4), (SEND_KEYS, 0, 8, 5), (SEND_KEYS, 0, 7, 1),
+    (SEND_KEYS, 0, 1, 0), (PREPARE, 0), (WAIT_TWIN, 0), (COMPARE, 0, 0, 2, True, True), (FINISH_ROWS, 0),
+    (WAIT, 2, 0), (TWIN, 2, 0), (WAIT_KEYS, 2), (SEND_KEYS, 2, 6, 2), (PREPARE, 2), (WAIT, 11, 0), (TWIN, 11, 0),
+    (WAIT_KEYS, 11), (SEND_KEYS, 11, 3, 0), (PREPARE, 11), (WAIT, 8, 0), (TWIN, 8, 0), (WAIT_KEYS, 8),
     (SEND_KEYS, 8, 10, 5), (PREPARE, 8), (WAIT, 7, 0), (TWIN, 7, 0), (WAIT_KEYS, 7), (SEND_KEYS, 7, 5, 3),
     (PREPARE, 7), (WAIT, 1, 0), (SEND, 0, 7, 5, 3), (SEND, 0, 2, 6, 2), (SEND, 2, 0, 11, 4), (SEND, 0, 11, 3, 0),
     (SEND, 1, 0, 7, 1), (SEND, 1, 0, 8, 5), (TWIN, 1, 0), (WAIT_KEYS, 1), (PREPARE, 1), (WAIT, 2, 1), (TWIN, 2, 1),

time: 37.7 us -> 40.7 us (1.080)
  Pallas kernels: 37 us -> 39.8 us
    pallas_call x1, Pallas kernels: 37 us -> 39.8 us  [body(): pl.pallas_call(kernel, out_shape=jax.ShapeDtypeStruct((1, size), jnp.floa...]
where the time goes in v6:
time: 40.7 us; the launch traced here: 40.4 us
  Pallas kernels  39.8 us (98%)
  local copies, waits for them, and re-layouts  0.56 us (1%)
    pallas_call x1, Pallas kernels, body(): pl.pallas_call(kernel, out_shape=jax.ShapeDtypeStruct((1, size), jnp.floa...  39.8 us

profile of v6, /device:TPU:1, one launch (start us, length us, event | category | flops | bytes accessed | tf_op | source)
XLA Modules:
  0.0 40.4 jit_solution(15540195584715042412)
XLA Ops:
  0.0 39.8 %nearest.1 = f32[1,256]{1,0:T(1,128)S(1)} custom-call(bf16[256,768]{1,0:T(8,128)(2,1)} %x_hbm.1, s32[1,256]{1,0:T(1,128)} %bitcast.4, s32[1,256]{1,0:T(1,128)} %bitcast.5), custom_call_target="tpu_custom_call" | custom-call | tf_op jit(solution)/shard_map/nearest/pallas_call | solution.py:261
  39.8 0.6 %copy.5 = f32[256]{0:T(256)} copy(f32[256]{0:T(256)S(1)} %bitcast.3) | data formatting | bytes 2048
